TPU v7x, 32 devices: a whole 2x2x4 slice. The times are simulated.
32 devices in a mesh: dp: 16 (over z, y, x), tensor: 2 (over core).
Axes of the slice: x: 2, y: 2, z: 4, core: 2. Of those that a mesh axis runs over, the one named last changes fastest.
Arguments:
- tokens: bfloat16 [16, 1024, 768], P('dp', 'tensor'), may hold values from -6 to 6
- lengths: int32 [16], replicated, may hold values from 576 to 1024, as said below
- drop_in: int32 [16, 2, 1024, 768], P('dp', None, 'tensor'), may hold values 0 or 1
- drop_attn: int32 [16, 2, 1024, 768], P('dp', None, 'tensor'), may hold values 0 or 1
- drop_ffn: int32 [16, 2, 1024, 768], P('dp', None, 'tensor'), may hold values 0 or 1
- qkv_weight: bfloat16 [768, 3, 768], P(None, None, 'tensor'), may hold values from -0.21875 to 0.21875
- out_weight: bfloat16 [768, 768], P('tensor'), may hold values from -6 to 6
- up_weight: bfloat16 [768, 3072], P(None, 'tensor'), may hold values from -0.21875 to 0.21875
- down_weight: bfloat16 [3072, 768], P('tensor'), may hold values from -0.109375 to 0.109375
- gain_first: float32 [768], replicated, may hold values from 0.5 to 1.5
- shift_first: float32 [768], replicated, may hold values from -0.5 to 0.5
- gain_second: float32 [768], replicated, may hold values from 0.5 to 1.5
- shift_second: float32 [768], replicated, may hold values from -0.46875 to 0.46875
- cotangent: bfloat16 [16, 2, 1024, 768], P('dp', None, 'tensor'), may hold values from -0.00063323975 to 0.00063323975
Outputs:
- layer_out: bfloat16 [16, 2, 1024, 768], P('dp', None, 'tensor')
- grad_tokens: float32 [16, 1024, 768], P('dp', 'tensor')
- grad_qkv: float32 [768, 3, 768], P(None, None, 'tensor')
- grad_out: float32 [768, 768], P('tensor')
- grad_up: float32 [768, 3072], P(None, 'tensor')
- grad_down: float32 [3072, 768], P('tensor')
- grad_gain_first: float32 [768], replicated
- grad_shift_first: float32 [768], replicated
- grad_gain_second: float32 [768], replicated
- grad_shift_second: float32 [768], replicated
- loss: float32 [], replicated
- alignment: float32 [], replicated
- uniformity: float32 [], replicated
Inputs may be any that keep to these rules, and one draw needn't show every extreme that they name: `lengths`: at least one pair is 1024 tokens long.
All inputs are finite; a program needn't handle non-finite values. No bound on the sum of `drop_in` or of `drop_attn` or of `drop_ffn` on one device may be relied on, other than what follows from the above.
Results may differ from a plain program's by a relative error of at most 0.019.
The roundings to bfloat16 on the way count: a program that leaves them out, or rounds other values in their place, can miss the bound.
Values may be sent and summed in bfloat16 or wider, within the bound.
A program may use at most 192 MiB of HBM per device.

v0:
```python
from functools import partial

import jax
import jax.numpy as jnp
from jax import lax
from jax.sharding import PartitionSpec as P

HEAD_DIM = 64


EXACT_PRECISION = lax.Precision.HIGHEST
KEEP_RATE = 0.9
SOFTMAX_WARMTH = 0.05
EPSILON = 1e-06
MASKED_SCORE = -1e30


def layer_norm(resid, gain_vec, shift_vec):
    row_mean = jnp.mean(resid, axis=-1, keepdims=True)
    centred = resid - row_mean
    row_var = jnp.mean(centred * centred, axis=-1, keepdims=True)
    return centred * lax.rsqrt(row_var + EPSILON) * gain_vec + shift_vec


def block_scores(query_block, keys, live_keys):
    scores = jnp.einsum(
        "qhd,khd->hqk", query_block, keys, preferred_element_type=jnp.float32
    ) * HEAD_DIM ** (-0.5)
    return jnp.where(live_keys[None, None, :], scores, MASKED_SCORE)


def attend(members):
    queries, keys, values, length = members
    full_len, heads_here, head_size = queries.shape
    block_rows = min(512, full_len)
    live_keys = jnp.arange(full_len, dtype=jnp.int32) < length

    def one_block(query_block):
        scores = block_scores(query_block, keys, live_keys)
        row_top = jnp.max(scores, axis=-1, keepdims=True)
        raw_weights = jnp.exp(scores - row_top)
        row_total = jnp.sum(raw_weights, axis=-1, keepdims=True)
        probs = raw_weights / row_total
        context = jnp.einsum(
            "hqk,khd->qhd", probs.astype(jnp.bfloat16), values, preferred_element_type=jnp.float32
        )
        return (context.astype(jnp.bfloat16), (row_top + jnp.log(row_total))[..., 0])

    blocks = queries.reshape(full_len // block_rows, block_rows, heads_here, head_size)
    context, log_total = lax.map(one_block, blocks)
    return (context.reshape(full_len, heads_here * head_size), log_total)


def attend_back(members):
    queries, keys, values, length, d_context, log_total = members
    full_len, heads_here, head_size = queries.shape
    block_rows = min(512, full_len)
    block_count = full_len // block_rows
    live_keys = jnp.arange(full_len, dtype=jnp.int32) < length
    scale = HEAD_DIM ** (-0.5)

    def one_block(running, parts):
        query_block, d_block, total_block = parts
        scores = block_scores(query_block, keys, live_keys)
        probs = jnp.exp(scores - total_block[..., None])
        d_probs = jnp.einsum("qhd,khd->hqk", d_block, values, preferred_element_type=jnp.float32)
        row_delta = jnp.sum(probs * d_probs, axis=-1, keepdims=True)
        d_scores = (probs * (d_probs - row_delta)).astype(jnp.bfloat16)
        d_queries = (
            jnp.einsum("hqk,khd->qhd", d_scores, keys, preferred_element_type=jnp.float32) * scale
        )
        d_keys = (
            running[0]
            + jnp.einsum("hqk,qhd->khd", d_scores, query_block, preferred_element_type=jnp.float32)
            * scale
        )
        d_values = running[1] + jnp.einsum(
            "hqk,qhd->khd", probs.astype(jnp.bfloat16), d_block, preferred_element_type=jnp.float32
        )
        return ((d_keys, d_values), d_queries)

    zeros = jnp.zeros(keys.shape, jnp.float32)
    query_blocks = queries.reshape(block_count, block_rows, heads_here, head_size)
    d_blocks = d_context.reshape(block_count, block_rows, heads_here, head_size)
    (d_keys, d_values), d_queries = lax.scan(
        one_block, (zeros, zeros), (query_blocks, d_blocks, log_total)
    )
    width = heads_here * head_size
    stacked = jnp.stack(
        [
            d_queries.reshape(full_len, width),
            d_keys.reshape(full_len, width),
            d_values.reshape(full_len, width),
        ],
        axis=1,
    )
    return stacked.astype(jnp.bfloat16)


def per_device(
    tokens,
    lengths,
    drop_in,
    drop_attn,
    drop_ffn,
    qkv_weight,
    out_weight,
    up_weight,
    down_weight,
    gain_first,
    shift_first,
    gain_second,
    shift_second,
    cotangent,
):
    pairs_here, local_len, width = tokens.shape
    tensor_count = lax.axis_size("tensor")
    data_count = lax.axis_size("dp")
    full_len = local_len * tensor_count
    pair_total = pairs_here * data_count
    data_index = lax.axis_index("dp")
    tensor_index = lax.axis_index("tensor")
    anchor_start = data_index * pairs_here
    own_lengths = lax.dynamic_slice_in_dim(lengths, anchor_start, pairs_here, 0)
    positions = tensor_index * local_len + jnp.arange(local_len, dtype=jnp.int32)
    live_rows = positions[None, :] < own_lengths[:, None]
    keep_in = drop_in.astype(jnp.float32)
    keep_attn = drop_attn.astype(jnp.float32)
    keep_ffn = drop_ffn.astype(jnp.float32)
    heads_here = qkv_weight.shape[2] // HEAD_DIM
    head_width = qkv_weight.shape[2]
    seq_count = pairs_here * 2
    view_lengths = jnp.repeat(own_lengths, 2)
    x_view = tokens.astype(jnp.float32)[:, None] * keep_in / KEEP_RATE
    x_low = x_view.astype(jnp.bfloat16)
    x_full = lax.all_gather(x_low, "tensor", axis=2, tiled=True)
    qkv = jnp.einsum(
        "pvtd,dce->pvtce", x_full, qkv_weight, preferred_element_type=jnp.float32
    ).astype(jnp.bfloat16)
    qkv_flat = qkv.reshape(seq_count, full_len, 3, head_width)
    queries = qkv_flat[:, :, 0].reshape(seq_count, full_len, heads_here, HEAD_DIM)
    keys = qkv_flat[:, :, 1].reshape(seq_count, full_len, heads_here, HEAD_DIM)
    values = qkv_flat[:, :, 2].reshape(seq_count, full_len, heads_here, HEAD_DIM)
    context, log_total = lax.map(attend, (queries, keys, values, view_lengths))
    context = context.reshape(pairs_here, 2, full_len, head_width)
    attn_terms = jnp.einsum(
        "pvtd,de->pvte", context, out_weight, preferred_element_type=jnp.float32
    )
    attn_branch = lax.psum_scatter(
        attn_terms.astype(jnp.bfloat16), "tensor", scatter_dimension=2, tiled=True
    ).astype(jnp.float32)
    r_one = x_view + attn_branch * keep_attn / KEEP_RATE
    h_one = layer_norm(r_one, gain_first, shift_first)
    h_low = h_one.astype(jnp.bfloat16)
    exact_gelu = partial(jax.nn.gelu, approximate=False)
    h_full = lax.all_gather(h_low, "tensor", axis=2, tiled=True)
    pre_act = jnp.einsum("pvtd,df->pvtf", h_full, up_weight, preferred_element_type=jnp.float32)
    activated = exact_gelu(pre_act).astype(jnp.bfloat16)
    ffn_terms = jnp.einsum(
        "pvtf,fd->pvtd", activated, down_weight, preferred_element_type=jnp.float32
    )
    ffn_branch = lax.psum_scatter(
        ffn_terms.astype(jnp.bfloat16), "tensor", scatter_dimension=2, tiled=True
    ).astype(jnp.float32)
    r_two = h_one + ffn_branch * keep_ffn / KEEP_RATE
    layer_rows = layer_norm(r_two, gain_second, shift_second)
    pooled_part = jnp.sum(jnp.where(live_rows[:, None, :, None], layer_rows, 0.0), axis=2)
    pooled_all = lax.all_gather(pooled_part, ("dp", "tensor"), axis=0, tiled=True)
    pooled_sum = jnp.sum(
        pooled_all.reshape(data_count, tensor_count, pairs_here, 2, width), axis=1
    ).reshape(pair_total, 2, width)
    all_lengths = lengths.astype(jnp.float32)
    targets = anchor_start + jnp.arange(pairs_here, dtype=jnp.int32)
    columns = jnp.arange(pair_total, dtype=jnp.int32)

    def contrast(summed):
        pooled = summed / all_lengths[:, None, None]
        unit_vectors = pooled * lax.rsqrt(
            jnp.sum(pooled * pooled, axis=-1, keepdims=True) + EPSILON
        )
        anchor_rows = lax.dynamic_slice_in_dim(unit_vectors[:, 0], anchor_start, pairs_here, 0)
        cosine_scores = (
            jnp.dot(anchor_rows, unit_vectors[:, 1].T, precision=EXACT_PRECISION) / SOFTMAX_WARMTH
        )
        row_top = jnp.max(cosine_scores, axis=1, keepdims=True)
        log_sum = row_top[:, 0] + jnp.log(jnp.sum(jnp.exp(cosine_scores - row_top), axis=1))
        positive = jnp.sum(
            jnp.where(columns[None, :] == targets[:, None], cosine_scores, 0.0), axis=1
        )
        return (jnp.sum(log_sum - positive), unit_vectors)

    loss_sum, contrast_back, unit_vectors = jax.vjp(contrast, pooled_sum, has_aux=True)
    grad_pool = contrast_back(jnp.float32(1.0))[0]
    first_dropout_view = unit_vectors[:, 0]
    own_first = lax.dynamic_slice_in_dim(first_dropout_view, anchor_start, pairs_here, 0)
    own_second = lax.dynamic_slice_in_dim(unit_vectors[:, 1], anchor_start, pairs_here, 0)
    gap = own_first - own_second
    align_sum = jnp.sum(gap * gap)
    own_norms = jnp.sum(own_first * own_first, axis=-1)
    sq_norms = jnp.sum(first_dropout_view * first_dropout_view, axis=-1)
    sq_dist = (
        own_norms[:, None]
        + sq_norms[None, :]
        - 2.0 * jnp.dot(own_first, first_dropout_view.T, precision=EXACT_PRECISION)
    )
    uniform_sum = jnp.sum(
        jnp.where(columns[None, :] != targets[:, None], jnp.exp(-2.0 * sq_dist), 0.0)
    )
    second_grad = lax.psum_scatter(grad_pool[:, 1], "dp", scatter_dimension=0, tiled=True)
    first_grad = lax.dynamic_slice_in_dim(grad_pool[:, 0], anchor_start, pairs_here, 0)
    pool_grad = jnp.stack([first_grad, second_grad], axis=1)
    d_layer = cotangent.astype(jnp.float32) + jnp.where(
        live_rows[:, None, :, None], pool_grad[:, :, None, :], 0.0
    )
    norm_two_out, norm_two_back = jax.vjp(layer_norm, r_two, gain_second, shift_second)
    d_r_two, grad_gain_b, grad_shift_b = norm_two_back(d_layer)
    g_two = (d_r_two * keep_ffn / KEEP_RATE).astype(jnp.bfloat16)
    gelu_out, gelu_back = jax.vjp(exact_gelu, pre_act)
    g_two_full = lax.all_gather(g_two, "tensor", axis=2, tiled=True)
    d_act = jnp.einsum("pvte,fe->pvtf", g_two_full, down_weight, preferred_element_type=jnp.float32)
    d_pre = gelu_back(d_act)[0].astype(jnp.bfloat16)
    down_grad_here = jnp.einsum(
        "pvtf,pvte->fe", activated, g_two_full, preferred_element_type=jnp.float32
    )
    up_grad_here = jnp.einsum("pvtd,pvtf->df", h_full, d_pre, preferred_element_type=jnp.float32)
    back_terms = jnp.einsum("pvtf,df->pvtd", d_pre, up_weight, preferred_element_type=jnp.float32)
    d_h_low = lax.psum_scatter(
        back_terms.astype(jnp.bfloat16), "tensor", scatter_dimension=2, tiled=True
    ).astype(jnp.float32)
    d_h_one = d_h_low + d_r_two
    norm_one_out, norm_one_back = jax.vjp(layer_norm, r_one, gain_first, shift_first)
    d_r_one, grad_gain_a, grad_shift_a = norm_one_back(d_h_one)
    g_one = (d_r_one * keep_attn / KEEP_RATE).astype(jnp.bfloat16)
    g_one_full = lax.all_gather(g_one, "tensor", axis=2, tiled=True)
    out_grad_here = jnp.einsum(
        "pvtd,pvte->de", context, g_one_full, preferred_element_type=jnp.float32
    )
    d_context = jnp.einsum(
        "pvte,de->pvtd", g_one_full, out_weight, preferred_element_type=jnp.float32
    ).astype(jnp.bfloat16)
    d_context = d_context.reshape(seq_count, full_len, heads_here, HEAD_DIM)
    d_qkv = lax.map(attend_back, (queries, keys, values, view_lengths, d_context, log_total))
    d_qkv = d_qkv.reshape(pairs_here, 2, full_len, 3, head_width)
    qkv_grad_here = jnp.einsum("pvtd,pvtce->dce", x_full, d_qkv, preferred_element_type=jnp.float32)
    input_terms = jnp.einsum(
        "pvtce,dce->pvtd", d_qkv, qkv_weight, preferred_element_type=jnp.float32
    )
    d_x_low = lax.psum_scatter(
        input_terms.astype(jnp.bfloat16), "tensor", scatter_dimension=2, tiled=True
    ).astype(jnp.float32)
    d_x_view = d_x_low + d_r_one
    grad_tokens = jnp.sum(d_x_view / KEEP_RATE * keep_in, axis=1)
    grad_qkv, grad_out, grad_up, grad_down = lax.psum(
        (qkv_grad_here, out_grad_here, up_grad_here, down_grad_here), "dp"
    )
    norm_grads = jnp.stack([grad_gain_a, grad_shift_a, grad_gain_b, grad_shift_b])
    statistics = jnp.stack([loss_sum, align_sum, uniform_sum])
    summed_norms, summed_stats = lax.psum((norm_grads, statistics), ("dp", "tensor"))
    summed_stats = summed_stats / tensor_count
    loss_mean = summed_stats[0] / pair_total
    alignment = summed_stats[1] / pair_total
    uniformity = jnp.log(summed_stats[2] / (pair_total * (pair_total - 1)))
    return (
        layer_rows.astype(jnp.bfloat16),
        grad_tokens,
        grad_qkv,
        grad_out,
        grad_up,
        grad_down,
        summed_norms[0],
        summed_norms[1],
        summed_norms[2],
        summed_norms[3],
        loss_mean,
        alignment,
        uniformity,
    )


def solution(mesh):
    in_specs = (
        P("dp", "tensor", None),
        P(),
        P("dp", None, "tensor", None),
        P("dp", None, "tensor", None),
        P("dp", None, "tensor", None),
        P(None, None, "tensor"),
        P("tensor", None),
        P(None, "tensor"),
        P("tensor", None),
        P(),
        P(),
        P(),
        P(),
        P("dp", None, "tensor", None),
    )
    out_specs = (
        P("dp", None, "tensor", None),
        P("dp", "tensor", None),
        P(None, None, "tensor"),
        P("tensor", None),
        P(None, "tensor"),
        P("tensor", None),
        P(),
        P(),
        P(),
        P(),
        P(),
        P(),
        P(),
    )
    return jax.shard_map(
        per_device, mesh=mesh, in_specs=in_specs, out_specs=out_specs, check_vma=False
    )
```

profile of v0, /device:TPU:0, one launch (start us, length us, event | category | flops | bytes accessed | tf_op | source)
XLA Modules:
  0.0 1055.1 jit_solution(13750709487045646821)
XLA Ops:
  13.9 14.3 %all-gather.7.cloned.1.call-done = bf16[1,2,1024,768]{3,2,1,0:T(8,128)(2,1)} async-done(((bf16[1,2,512,768]{3,2,1,0:T(8,128)(2,1)}), bf16[1,2,1024,768]{3,2,1,0:T(8,128)(2,1)}) %all-gather.7.cloned.1.call-update) | async-done | bytes 3145744 | tf_op jit(solution)/shard_map/all_gather | solution.py:136
  37.4 76.8 %while.51 = (s32[]{:T(128)}, bf16[2,1024,384]{1,2,0:T(8,128)(2,1)}, f32[2,2,6,512]{3,2,1,0:T(8,128)S(1)}, bf16[2,1024,6,64]{1,3,2,0:T(8,128)(2,1)}, bf16[2,1024,...) while((s32[]{:T(128)}, bf16[2,1024,384]{1,2,0:T(8,128)(2,1)}, ...), condition=%wide.region_5.6_spmd, body=%wide.region_0.5_spmd.sunk | while | flops 843249664 | bytes 62310232 | solution.py:144
  47.1 22.5 %while.54 = (s32[]{:T(128)}, bf16[2,512,6,64]{1,3,2,0:T(8,128)(2,1)}, f32[2,6,512]{2,1,0:T(8,128)S(1)}, bf16[2,512,6,64]{1,3,2,0:T(8,128)(2,1)}, bf16[1024,6,64]...) while((s32[]{:T(128)}, bf16[2,512,6,64]{1,3,2,0:T(8,128)(2,1)}, ...), condition=%wide.region_4.4_spmd.clone, body=%wide.region_1.3_spmd.clone.sunk | while | flops 843249664 | bytes 43369592 | solution.py:50
  85.4 22.5 %while.54 = (s32[]{:T(128)}, bf16[2,512,6,64]{1,3,2,0:T(8,128)(2,1)}, f32[2,6,512]{2,1,0:T(8,128)S(1)}, bf16[2,512,6,64]{1,3,2,0:T(8,128)(2,1)}, bf16[1024,6,64]...) while((s32[]{:T(128)}, bf16[2,512,6,64]{1,3,2,0:T(8,128)(2,1)}, ...), condition=%wide.region_4.4_spmd.clone, body=%wide.region_1.3_spmd.clone.sunk | while | flops 843249664 | bytes 43369592 | solution.py:50
  119.4 12.2 %reduce-scatter.5.cloned.1.call-done = bf16[1,2,512,768]{3,2,1,0:T(8,128)(2,1)} async-done(((bf16[1,2,1024,768]{3,2,1,0:T(8,128)(2,1)}), bf16[1,2,512,768]{3,2,1,0:T(8,128)(2,1)}) %reduce-scatter.5.cloned.1.call-update) | async-done | bytes 1572880 | tf_op jit(solution)/shard_map/reduce_scatter | solution.py:149
  140.1 13.0 %all-gather.9.cloned.1.call-done = bf16[1,2,1024,768]{3,2,1,0:T(8,128)(2,1)} async-done(((bf16[1,2,512,768]{3,2,1,0:T(8,128)(2,1)}), bf16[1,2,1024,768]{3,2,1,0:T(8,128)(2,1)}) %all-gather.9.cloned.1.call-update) | async-done | bytes 3145744 | tf_op jit(solution)/shard_map/all_gather | solution.py:156
  153.1 10.7 %fusion.63 = (u8[1024,1536]{1,0:T(8,128)(4,1)S(1)}, u8[1024,1536]{1,0:T(8,128)(4,1)S(1)}, f32[2,1024,1536]{2,1,0:T(8,128)S(1)}) fusion(bf16[768,1536]{1,0:T(8,128)(2,1)S(1)} %copy-done, bf16[1,2,1024,768]{3,2,1,0:T(8,128)(2,1)} %all-gather.9.cloned.1.call-done), kind=kOutput, calls=%fused_computation.122 | convolution fusion | flops 4869586944 | bytes 21233664 | tf_op jit(solution)/shard_map/pvtd,df->pvtf/dot_general | solution.py:157
  163.8 29.6 %multiply_convert_fusion.1 = (bf16[2,1024,1536]{2,1,0:T(8,128)(2,1)S(1)}, f32[2,1024,1536]{2,1,0:T(8,128)}) fusion(f32[2,1024,1536]{2,1,0:T(8,128)S(1)} %get-tuple-element.429, u8[1024,1536]{1,0:T(8,128)(4,1)S(1)} %get-tuple-element.308, u8[1024,1536]{1,0:T(8,128)(4,1)S(1)} %get-tuple-element.307), kind=kLoop, calls=%fused_computation.67 | loop fusion | flops 220200960 | bytes 34603008 | tf_op jit(solution)/shard_map/convert_element_type | solution.py:158
  204.4 10.3 reduce-scatter.7.cloned.1.call-done
  221.8 42.2 %all-gather.1 = f32[32,2,768]{2,1,0:T(2,128)S(1)} all-gather(f32[1,2,768]{2,1,0:T(2,128)S(1)} %bitcast.307), channel_id=2, replica_groups=mesh['dp'=16,'tensor'=2] {'dp','tensor'}, dimensions={0}, use_global_device_ids=true | all-gather | bytes 202752 | tf_op jit(solution)/shard_map/all_gather | solution.py:168
  271.9 71.8 %all-reduce.2 = f32[16,768]{1,0:T(8,128)S(1)} all-reduce(f32[16,768]{1,0:T(8,128)S(1)} %bitcast.306), channel_id=5, replica_groups=mesh['dp'=16,'tensor'=2] {'dp'}, use_global_device_ids=true, to_apply=%region_20.21.clone | all-reduce | flops 12288 | bytes 98304
  362.1 16.2 %add_convert_fusion = bf16[2,1024,1536]{2,1,0:T(8,128)(2,1)S(1)} fusion(f32[2,1024,1536]{2,1,0:T(8,128)} %get-tuple-element.404, f32[2,1024,1536]{2,1,0:T(8,128)} %copy-done.15, bf16[1,2,1024,768]{3,2,1,0:T(8,128)(2,1)} %all-gather.11.cloned.1.call-done, bf16[1536,768]{1,0:T(8,128)(2,1)} %param.30), kind=kOutput, calls=%fused_computation.66 | convolution fusion | flops 4875878400 | bytes 36962304 | tf_op jit(solution)/shard_map/pvte,fe->pvtf/dot_general | solution.py:220
  387.5 12.2 %reduce-scatter.9.cloned.1.call-done = bf16[1,2,512,768]{3,2,1,0:T(8,128)(2,1)} async-done(((bf16[1,2,1024,768]{3,2,1,0:T(8,128)(2,1)}), bf16[1,2,512,768]{3,2,1,0:T(8,128)(2,1)}) %reduce-scatter.9.cloned.1.call-update) | async-done | bytes 1572880 | tf_op jit(solution)/shard_map/reduce_scatter | solution.py:227
  411.7 13.4 %all-gather.13.cloned.1.call-done = bf16[1,2,1024,768]{3,2,1,0:T(8,128)(2,1)} async-done(((bf16[1,2,512,768]{3,2,1,0:T(8,128)(2,1)}), bf16[1,2,1024,768]{3,2,1,0:T(8,128)(2,1)}) %all-gather.13.cloned.1.call-update) | async-done | bytes 3145744 | tf_op jit(solution)/shard_map/all_gather | solution.py:234
  429.5 165.1 %while.53 = (s32[]{:T(128)}, bf16[2,1024,3,384]{1,3,2,0:T(8,128)(2,1)}, bf16[2,1024,6,64]{1,3,2,0:T(8,128)(2,1)}, bf16[2,1024,6,64]{1,3,2,0:T(8,128)(2,1)}, f32[...) while((s32[]{:T(128)}, ...), condition=%wide.region_30.31_spmd, body=%wide.region_26.30_spmd.sunk | while | flops 2070476800 | bytes 241190640 | solution.py:242
  436.8 69.6 %while.55 = (s32[]{:T(128)}, f32[1024,6,64]{0,2,1:T(8,128)S(1)}, f32[1024,6,64]{0,2,1:T(8,128)}, bf16[2,512,6,64]{1,3,2,0:T(8,128)(2,1)}, bf16[2,512,6,64]{1,3,2...) while((s32[]{:T(128)}, f32[1024,6,64]{0,2,1:T(8,128)S(1)}, ...), condition=%wide.region_29.29_spmd.clone, body=%wide.region_27.28_spmd.clone.sunk | while | flops 2062612480 | bytes 215581488 | solution.py:85
  481.1 9.4 multiply_convert_fusion.5
  519.1 69.6 %while.55 = (s32[]{:T(128)}, f32[1024,6,64]{0,2,1:T(8,128)S(1)}, f32[1024,6,64]{0,2,1:T(8,128)}, bf16[2,512,6,64]{1,3,2,0:T(8,128)(2,1)}, bf16[2,512,6,64]{1,3,2...) while((s32[]{:T(128)}, f32[1024,6,64]{0,2,1:T(8,128)S(1)}, ...), condition=%wide.region_29.29_spmd.clone, body=%wide.region_27.28_spmd.clone.sunk | while | flops 2062612480 | bytes 215581488 | solution.py:85
  529.2 9.4 multiply_convert_fusion.5
  563.4 9.4 multiply_convert_fusion.5
  603.6 9.7 convolution_bitcast_fusion
  613.3 10.1 convolution_bitcast_fusion.1
  639.3 45.3 %all-reduce.3 = (f32[4,768]{1,0:T(4,128)S(1)}, f32[3]{0:T(128)S(1)}) all-reduce(f32[4,768]{1,0:T(4,128)S(1)} %pad_maximum_fusion, f32[3]{0:T(128)S(1)} %pad_maximum_fusion.1), channel_id=1, replica_groups=mesh['dp'=16,'tensor'=2] {'dp','tensor'}, use_global_device_ids=true, to_apply=%region_41.42 | all-reduce | flops 3075 | bytes 24600 | tf_op jit(solution)/shard_map/psum | solution.py:258
  693.2 341.0 %all-reduce.7.cloned.1.call-done = (f32[768,3,384]{2,0,1:T(8,128)}, f32[384,768]{1,0:T(8,128)}, f32[768,1536]{1,0:T(8,128)}, f32[1536,768]{1,0:T(8,128)}) async-done(((f32[768,3,384]{2,0,1:T(8,128)}, f32[384,768]{1,0:T(8,128)}, f32[768,1536]{1,0:T(8,128)}, f32[1536,768]{1,0:T(8,128)}), (f32[768,3,384]{2,0,1:T(8,128)}, f32[384,768]{1,0:T(8,128)}, f32[768,1536]{1,0:T(8,128)}, ...) | async-done | bytes 14155792 | tf_op jit(solution)/shard_map/psum | solution.py:253
  (352 shorter events, 349.6 us)
Async XLA Ops:
  7.2 145.9 %copy-start = (bf16[768,1536]{1,0:T(8,128)(2,1)S(1)}, bf16[768,1536]{1,0:T(8,128)(2,1)}, u32[]{:S(2)}) copy-start(bf16[768,1536]{1,0:T(8,128)(2,1)} %param.29) | copy-start | bytes 7077892
  7.2 21.0 %all-gather.7.cloned.1.call-start = ((), (), s32[]{:S(2)}) async-start(), calls=%async_computation.4 | async-start | bytes 4718592 | tf_op jit(solution)/shard_map/all_gather | solution.py:136
  13.2 118.3 %reduce-scatter.5.cloned.1.call-start = ((), (), s32[]{:S(2)}) async-start(), calls=%async_computation.5 | async-start | bytes 4718592 | tf_op jit(solution)/shard_map/reduce_scatter | solution.py:149
  119.3 33.8 %all-gather.9.cloned.1.call-start = ((), (), s32[]{:S(2)}) async-start(), calls=%async_computation.6 | async-start | bytes 4718592 | tf_op jit(solution)/shard_map/all_gather | solution.py:156
  139.6 75.1 %reduce-scatter.7.cloned.1.call-start = ((), (), s32[]{:S(2)}) async-start(), calls=%async_computation.7 | async-start | bytes 4718592 | tf_op jit(solution)/shard_map/reduce_scatter | solution.py:162
  163.8 29.6 %copy-start.15 = (f32[2,1024,1536]{2,1,0:T(8,128)}, f32[2,1024,1536]{2,1,0:T(8,128)S(1)}, u32[]{:S(2)}) copy-start(f32[2,1024,1536]{2,1,0:T(8,128)S(1)} %get-tuple-element.429) | copy-start | bytes 37748740
  163.8 32.3 %copy-start.39 = (bf16[1536,768]{1,0:T(8,128)(2,1)S(1)}, bf16[1536,768]{1,0:T(8,128)(2,1)}, u32[]{:S(2)}) copy-start(bf16[1536,768]{1,0:T(8,128)(2,1)} %param.30) | copy-start | bytes 7077892
  202.5 159.6 %all-gather.11.cloned.1.call-start = ((), (), s32[]{:S(2)}) async-start(), calls=%async_computation.8 | async-start | bytes 4718592 | tf_op jit(solution)/shard_map/all_gather | solution.py:219
  354.0 45.7 %reduce-scatter.9.cloned.1.call-start = ((), (), s32[]{:S(2)}) async-start(), calls=%async_computation.9 | async-start | bytes 4718592 | tf_op jit(solution)/shard_map/reduce_scatter | solution.py:227
  387.5 37.6 %all-gather.13.cloned.1.call-start = ((), (), s32[]{:S(2)}) async-start(), calls=%async_computation.10 | async-start | bytes 4718592 | tf_op jit(solution)/shard_map/all_gather | solution.py:234
  409.9 15.1 %copy-start.41 = (bf16[384,768]{1,0:T(8,128)(2,1)S(1)}, bf16[384,768]{1,0:T(8,128)(2,1)}, u32[]{:S(2)}) copy-start(bf16[384,768]{1,0:T(8,128)(2,1)} %param.28) | copy-start | bytes 1769476
  411.6 276.2 %reduce-scatter.11.cloned.1.call-start = ((), (), s32[]{:S(2)}) async-start(), calls=%async_computation.11 | async-start | bytes 4718592 | tf_op jit(solution)/shard_map/reduce_scatter | solution.py:248
  438.6 8.3 copy-start.2
  456.3 10.7 %copy-start.3 = (f32[6,512,1024]{2,1,0:T(8,128)S(1)}, f32[6,512,1024]{2,1,0:T(8,128)}, u32[]{:S(2)}) copy-start(f32[6,512,1024]{2,1,0:T(8,128)} %copy-done.2) | copy-start | bytes 37748740 | tf_op jit(solution)/shard_map/while/body/eval_jaxpr/while
  472.8 8.3 copy-start.2
  490.5 10.7 %copy-start.3 = (f32[6,512,1024]{2,1,0:T(8,128)S(1)}, f32[6,512,1024]{2,1,0:T(8,128)}, u32[]{:S(2)}) copy-start(f32[6,512,1024]{2,1,0:T(8,128)} %copy-done.2) | copy-start | bytes 37748740 | tf_op jit(solution)/shard_map/while/body/eval_jaxpr/while
  538.6 10.7 %copy-start.3 = (f32[6,512,1024]{2,1,0:T(8,128)S(1)}, f32[6,512,1024]{2,1,0:T(8,128)}, u32[]{:S(2)}) copy-start(f32[6,512,1024]{2,1,0:T(8,128)} %copy-done.2) | copy-start | bytes 37748740 | tf_op jit(solution)/shard_map/while/body/eval_jaxpr/while
  555.1 8.3 copy-start.2
  572.8 10.7 %copy-start.3 = (f32[6,512,1024]{2,1,0:T(8,128)S(1)}, f32[6,512,1024]{2,1,0:T(8,128)}, u32[]{:S(2)}) copy-start(f32[6,512,1024]{2,1,0:T(8,128)} %copy-done.2) | copy-start | bytes 37748740 | tf_op jit(solution)/shard_map/while/body/eval_jaxpr/while
  603.5 430.6 %all-reduce.7.cloned.1.call-start = ((), (), s32[]{:S(2)}) async-start(), calls=%async_computation.12 | async-start | bytes 28311552 | tf_op jit(solution)/shard_map/psum | solution.py:253
  603.6 9.7 copy-start.37
  613.3 10.1 copy-start.38
  613.3 10.1 copy-start.40
  634.3 53.5 %copy-start.28 = (f32[2,512]{1,0:T(2,128)S(1)}, f32[2,512]{1,0:T(2,128)}, u32[]{:S(2)}) copy-start(f32[2,512]{1,0:T(2,128)} %copy-done.27) | copy-start | bytes 12292
  (60 other events, 199.9 us)
Sparse Core Ops, SparseCore 0:
  13.4 14.8 all-gather.6
  119.4 12.0 reduce-scatter.4
  139.8 13.2 all-gather.8
  202.6 12.0 reduce-scatter.6
  354.1 7.9 all-gather.10
  387.6 12.0 reduce-scatter.8
  411.7 13.2 all-gather.12
  603.7 12.0 reduce-scatter.10
  634.4 399.6 all-reduce.6
where the time goes:
time: 1060 us
  waiting for transfers between devices  425 us (40%)
  matrix products  224 us (21%)
  blocking collectives  159 us (15%)
  other arithmetic  140 us (13%)
  local copies, waits for them, and re-layouts  81.4 us (8%)
  between operations  24 us (2%)
    psum x1, waiting for transfers between devices, per_device(): lax.psum((qkv_grad_here, out_grad_here, up_grad_here, down_grad_here), 'dp')  341 us
    unnamed x1, blocking collectives  71.8 us
    psum x1, blocking collectives, per_device(): lax.psum((norm_grads, statistics), ('dp', 'tensor'))  45.3 us
    all_gather x1, blocking collectives, per_device(): lax.all_gather(pooled_part, ('dp', 'tensor'), axis=0, tiled=True)  42.2 us
    convert_element_type x4, other arithmetic, one_block(): d_scores = (probs * (d_probs - row_delta)).astype(jnp.bfloat16)  37.7 us
    convert_element_type x1, other arithmetic, per_device(): activated = exact_gelu(pre_act).astype(jnp.bfloat16)  29.6 us
    dot_general x4, matrix products, one_block(): jnp.einsum('qhd,khd->hqk', d_block, values, preferred_element_type=jnp.fl...  28.2 us
    dot_general x4, matrix products, one_block(): jnp.einsum('hqk,khd->qhd', d_scores, keys, preferred_element_type=jnp.flo...  25.5 us
  transfers between devices with their start and end apart: 9, of which 8 were waited for; matrix products, arithmetic and copies ran while one was open for 4% of the time, Pallas kernels for 0%

commit v1 on v0

v1 whole, which is shorter than its diff:
```python
import functools
import math

import jax
import jax.numpy as jnp
from jax import lax
from jax.experimental import pallas as pl
from jax.experimental.pallas import tpu as pltpu
from jax.sharding import PartitionSpec as P

HEAD_DIM = 64
INV_KEEP = 1.0 / 0.9
SOFTMAX_WARMTH = 0.05
EPSILON = 1e-06
MASKED_SCORE = -1e30
MESH = pl.DeviceIdType.MESH
F32 = jnp.float32
BF16 = jnp.bfloat16
VMEM_LIMIT = 60 * 2**20
HIGHEST = lax.Precision.HIGHEST

TAIL_P = 0.3
TAIL = (
    0.11962929778234735,
    0.12075397394392673,
    0.09991336806236217,
    0.1285620774207718,
    -0.05368457414666341,
    0.20635459819946347,
    -0.15720376083821283,
    0.03567494667807555,
)


def dot_nn(a, b):
    return jnp.dot(a, b, preferred_element_type=F32)


def dot_nt(a, b):
    return lax.dot_general(a, b, (((1,), (1,)), ((), ())), preferred_element_type=F32)


def dot_tn(a, b):
    return lax.dot_general(a, b, (((0,), (0,)), ((), ())), preferred_element_type=F32)


def gelu_pair(x):
    z = jnp.abs(x)
    bell = jnp.exp(x * x * -0.5)
    t = 1.0 / (1.0 + TAIL_P * z)
    acc = jnp.full_like(t, TAIL[-1])
    for c in TAIL[-2::-1]:
        acc = acc * t + c
    tail = acc * t * bell
    cdf = jnp.where(x < 0.0, tail, 1.0 - tail)
    return x * cdf, cdf + x * (bell * (1.0 / math.sqrt(2.0 * math.pi)))


def split_three(v):
    hi = v.astype(BF16).astype(F32)
    rest = v - hi
    mid = rest.astype(BF16).astype(F32)
    return hi, mid, rest - mid


def front_kernel(
    lens, tok, d_in, d_at, d_ff, cot, wq, wo, wu, wd,
    x0_o, ma_o, mf_o, cot_o, wq_o, wo_o, wu_o, wd_o, qkv_o, qb_o, ctx_o,
    xv, xl, wv, qs, ms, tokv, st, qbv, ctxv, in_sem, loc_sem, send_sem, recv_sem, out_sem,
):
    d = lax.axis_index("dp")
    t = lax.axis_index("tensor")
    other = 1 - t
    peer = (d, other)
    loc = tok.shape[0]
    full = 2 * loc
    half_w = wq.shape[1]
    hw = half_w // 3
    pairs = hw // 128

    barrier = pltpu.get_barrier_semaphore()
    pl.semaphore_signal(barrier, inc=1, device_id=peer, device_id_type=MESH)

    loads = [
        pltpu.make_async_copy(tok, tokv, in_sem.at[0]),
        pltpu.make_async_copy(d_in, ms.at[0], in_sem.at[1]),
        pltpu.make_async_copy(wq, wv.at[t], in_sem.at[2]),
        pltpu.make_async_copy(d_at, ms.at[1], in_sem.at[3]),
        pltpu.make_async_copy(d_ff, ms.at[2], in_sem.at[4]),
    ]
    for c in loads:
        c.start()
    own_rows = pl.ds(pl.multiple_of(t * loc, loc), loc)

    local = [
        pltpu.make_async_copy(cot.at[t], cot_o.at[own_rows], loc_sem.at[0]),
        pltpu.make_async_copy(wo, wo_o.at[t], loc_sem.at[1]),
        pltpu.make_async_copy(wu, wu_o.at[t], loc_sem.at[2]),
        pltpu.make_async_copy(wd, wd_o.at[t], loc_sem.at[3]),
        pltpu.make_async_copy(wq, wq_o.at[t], loc_sem.at[4]),
    ]

    def remote(i, src, dst):
        return pltpu.make_async_remote_copy(
            src_ref=src, dst_ref=dst, send_sem=send_sem.at[i], recv_sem=recv_sem.at[i],
            device_id=peer, device_id_type=MESH,
        )

    pl.semaphore_wait(barrier, 1)
    send_wq = remote(0, wq, wv.at[t])
    send_wq.start()
    loads[0].wait()
    loads[1].wait()
    st[0] = jnp.where(ms[0, other] != 0, tokv[...].astype(F32), 0.0).astype(BF16)
    send_x = remote(1, st.at[0], xv.at[own_rows])
    send_x.start()
    own_x = jnp.where(ms[0, t] != 0, tokv[...].astype(F32), 0.0)
    xv[own_rows, :] = own_x.astype(BF16)
    xl[own_rows, :] = (own_x * INV_KEEP).astype(BF16)
    for c in local:
        c.start()
    loads[3].wait()
    st[1] = ms[1, other].astype(F32).astype(BF16)
    st[2] = ms[1, t].astype(F32).astype(BF16)
    loads[4].wait()
    st[3] = ms[2, other].astype(F32).astype(BF16)
    st[4] = ms[2, t].astype(F32).astype(BF16)
    sends = [
        remote(2, wo, wo_o.at[t]),
        remote(3, st.at[1], ma_o.at[own_rows]),
        remote(4, wu, wu_o.at[t]),
        remote(5, wd, wd_o.at[t]),
        remote(6, st.at[3], mf_o.at[own_rows]),
        remote(7, cot.at[other], cot_o.at[own_rows]),
        remote(8, wq, wq_o.at[t]),
    ]
    for c in sends:
        c.start()
    more = [
        pltpu.make_async_copy(st.at[2], ma_o.at[own_rows], loc_sem.at[5]),
        pltpu.make_async_copy(st.at[4], mf_o.at[own_rows], loc_sem.at[6]),
    ]
    for c in more:
        c.start()

    loads[2].wait()
    send_wq.wait_recv()
    send_x.wait_recv()
    oth_rows = pl.ds(pl.multiple_of(other * loc, loc), loc)
    xl[oth_rows, :] = (xv[oth_rows, :].astype(F32) * INV_KEEP).astype(BF16)
    save_x = pltpu.make_async_copy(xv, x0_o, loc_sem.at[7])
    save_x.start()

    for h in range(2):
        for c in range(3):
            def project(b, _, h=h, c=c):
                rows = pl.ds(pl.multiple_of(b * 512, 512), 512)
                qs[h, rows, c * hw : (c + 1) * hw] = dot_nn(
                    xl[rows, :], wv[h, :, c * hw : (c + 1) * hw]
                ).astype(BF16)
                return 0

            lax.fori_loop(0, full // 512, project, 0)
    save_qkv = pltpu.make_async_copy(qs, qkv_o, loc_sem.at[8])
    save_qkv.start()

    length = lens[d]
    bias = jnp.where(
        lax.broadcasted_iota(jnp.int32, (full, 128), 0) < length, 0.0, MASKED_SCORE
    )
    lane = lax.broadcasted_iota(jnp.int32, (full, 128), 1)
    lane_q = lax.broadcasted_iota(jnp.int32, (512, 128), 1)

    def out_copies(i):
        return [
            pltpu.make_async_copy(qbv.at[pl.ds(2 * i, 2)], qb_o.at[pl.ds(2 * i, 2)], out_sem.at[0, i]),
            pltpu.make_async_copy(ctxv.at[i], ctx_o.at[i], out_sem.at[1, i]),
        ]

    def head_pair(i, _):
        h = i // pairs
        off = (i - h * pairs) * 128

        def part(c):
            return qs[h, :, pl.ds(pl.multiple_of(c * hw + off, 128), 128)].astype(F32)

        q2 = part(0) * HEAD_DIM**-0.5
        k2 = part(1)
        v2 = part(2)
        keys, vals, ques = [], [], []
        for a in range(2):
            own = (lane < 64) if a == 0 else (lane >= 64)
            first = 64 if a == 0 else 0
            keys.append(jnp.where(own, k2, jnp.where(lane == first, bias, 0.0)).astype(BF16))
            ques.append(jnp.where(own, q2, jnp.where(lane == first, 1.0, 0.0)).astype(BF16))
            vals.append(jnp.where(own, v2, 1.0).astype(BF16))
        for b in range(full // 512):
            rows = slice(b * 512, (b + 1) * 512)
            tops, outs = [], []
            for a in range(2):
                s = dot_nt(ques[a][rows], keys[a])
                top = jnp.max(s, axis=1, keepdims=True)
                p = jnp.exp(s - top).astype(BF16)
                outs.append(dot_nn(p, vals[a]))
                tops.append(top)
            low_half = lane_q < 64
            num = jnp.where(low_half, outs[0], outs[1])
            den = pltpu.roll(jnp.where(low_half, outs[1], outs[0]), 64, 1)
            ctxv[i, rows, :] = num / den
            for a in range(2):
                hi, mid, lo = split_three(tops[a] + jnp.log(outs[a]))
                own = low_half if a == 0 else jnp.logical_not(low_half)
                first = 64 if a == 0 else 0
                extra = jnp.where(
                    lane_q == first, hi,
                    jnp.where(lane_q == first + 1, mid,
                              jnp.where(lane_q == first + 2, lo,
                                        jnp.where(lane_q == first + 3, 1.0, 0.0))),
                )
                qbv[2 * i + a, rows, :] = jnp.where(own, q2[rows], extra).astype(BF16)
        for c in out_copies(i):
            c.start()
        return 0

    lax.fori_loop(0, 2 * pairs, head_pair, 0)

    def drain(i, _):
        for c in out_copies(i):
            c.wait()
        return 0

    lax.fori_loop(0, 2 * pairs, drain, 0)
    send_wq.wait_send()
    send_x.wait_send()
    for c in sends:
        c.wait()
    for c in local + more + [save_x, save_qkv]:
        c.wait()


def front(lengths, tok, d_in, d_at, d_ff, cot, wq, wo, wu, wd):
    loc, width = tok.shape
    full = 2 * loc
    half_w = wq.shape[1]
    groups = width // 128
    sds = jax.ShapeDtypeStruct
    anyspec = pl.BlockSpec(memory_space=pl.ANY)
    outs = [
        sds((full, width), BF16), sds((full, width), BF16), sds((full, width), BF16),
        sds((full, width), BF16),
        sds((2,) + wq.shape, BF16), sds((2,) + wo.shape, BF16), sds((2,) + wu.shape, BF16),
        sds((2,) + wd.shape, BF16),
        sds((2, full, half_w), BF16), sds((2 * groups, full, 128), BF16),
        sds((groups, full, 128), F32),
    ]
    return pl.pallas_call(
        front_kernel,
        out_shape=outs,
        in_specs=[pl.BlockSpec(memory_space=pltpu.SMEM)] + [anyspec] * 9,
        out_specs=[anyspec] * len(outs),
        scratch_shapes=[
            pltpu.VMEM((full, width), BF16), pltpu.VMEM((full, width), BF16),
            pltpu.VMEM((2,) + wq.shape, BF16), pltpu.VMEM((2, full, half_w), BF16),
            pltpu.VMEM((3, 2, loc, width), jnp.int32), pltpu.VMEM((loc, width), BF16),
            pltpu.VMEM((5, loc, width), BF16),
            pltpu.VMEM((2 * groups, full, 128), BF16), pltpu.VMEM((groups, full, 128), F32),
            pltpu.SemaphoreType.DMA((5,)), pltpu.SemaphoreType.DMA((9,)),
            pltpu.SemaphoreType.DMA((9,)), pltpu.SemaphoreType.DMA((9,)),
            pltpu.SemaphoreType.DMA((2, groups)),
        ],
        compiler_params=pltpu.CompilerParams(
            collective_id=0, has_side_effects=True, vmem_limit_bytes=VMEM_LIMIT
        ),
        name="front",
    )(lengths, tok, d_in, d_at, d_ff, cot, wq, wo, wu, wd)


CH = 512


def middle_kernel(
    lens, lens_b, vecs, ctx, x0, ma, mf, cot, wo, wu, wd,
    lay_o, loss_o, gd_o, gu_o, go_o, ng_o, dr1_o, dob_o,
    ctxv, x0v, mav, mfv, cotv, wov, wuv, wdv,
    n1, n2, rs1, rs2, hl, act, dg, g2, dr2, yb, sbuf, pool_all, gch, uch, dov, facc,
    in_sem, lay_sem, send_sem, recv_sem, ch_sem, out_sem,
):
    d = lax.axis_index("dp")
    t = lax.axis_index("tensor")
    other = 1 - t
    peer = (d, other)
    n_dp = lax.axis_size("dp")
    n_dev = 2 * n_dp
    full, width = x0v.shape
    loc = full // 2
    groups = width // 128
    ff_half = wuv.shape[2]
    n_ch = 2 * ff_half // CH
    per_half = ff_half // CH
    me = d * 2 + t

    barrier = pltpu.get_barrier_semaphore()

    def greet(k, _):
        lin = lax.rem(me + k, n_dev)
        pl.semaphore_signal(
            barrier, inc=1, device_id=(lin // 2, lax.rem(lin, 2)), device_id_type=MESH
        )
        return 0

    lax.fori_loop(1, n_dev, greet, 0)

    srcs = (ctx, wo, x0, ma, wu, wd, mf, cot)
    dsts = (ctxv, wov, x0v, mav, wuv, wdv, mfv, cotv)
    loads = [pltpu.make_async_copy(s, v, in_sem.at[i]) for i, (s, v) in enumerate(zip(srcs, dsts))]
    for c in loads:
        c.start()
    gain1, shift1, gain2, shift2 = (vecs[i : i + 1, :] for i in range(4))
    length = lens[d]

    for c in loads[:4]:
        c.wait()

    def norm_one(b, _):
        rows = pl.ds(pl.multiple_of(b * 256, 256), 256)
        c2 = jnp.concatenate([ctxv[g, rows, :].astype(BF16) for g in range(groups)], axis=1)
        branch = dot_nn(c2, wov[...])
        r = (x0v[rows, :].astype(F32) + branch * mav[rows, :].astype(F32)) * INV_KEEP
        cen = r - jnp.mean(r, axis=1, keepdims=True)
        rstd = lax.rsqrt(jnp.mean(cen * cen, axis=1, keepdims=True) + EPSILON)
        n = cen * rstd
        n1[rows, :] = n
        rs1[rows, :] = jnp.broadcast_to(rstd, (256, 128))
        hl[rows, :] = (n * gain1 + shift1).astype(BF16)
        return 0

    lax.fori_loop(0, full // 256, norm_one, 0)
    for c in loads[4:]:
        c.wait()

    def ffn(b, pooled):
        rows = pl.ds(pl.multiple_of(b * 512, 512), 512)
        for j in range(n_ch):
            h, o = j // per_half, (j % per_half) * CH
            pre = dot_nn(hl[rows, :], wuv[h, :, o : o + CH])
            a, da = gelu_pair(pre)
            ab = a.astype(BF16)
            act[rows, j * CH : (j + 1) * CH] = ab
            dg[rows, j * CH : (j + 1) * CH] = da.astype(BF16)
            term = dot_nn(ab, wdv[j * CH : (j + 1) * CH, :])
            if j == 0:
                facc[...] = term
            else:
                facc[...] += term
        for s in range(2):
            sub = pl.ds(pl.multiple_of(b * 512 + s * 256, 256), 256)
            r = n1[sub, :] * gain1 + shift1 + facc[s * 256 : (s + 1) * 256, :] * (
                mfv[sub, :].astype(F32) * INV_KEEP
            )
            cen = r - jnp.mean(r, axis=1, keepdims=True)
            rstd = lax.rsqrt(jnp.mean(cen * cen, axis=1, keepdims=True) + EPSILON)
            n = cen * rstd
            n2[sub, :] = n
            rs2[sub, :] = jnp.broadcast_to(rstd, (256, 128))
            y = n * gain2 + shift2
            yb[sub, :] = y.astype(BF16)
            pos = lax.broadcasted_iota(jnp.int32, (256, width), 0) + (b * 512 + s * 256)
            pooled = pooled + jnp.sum(jnp.where(pos < length, y, 0.0), axis=0, keepdims=True)
        return pooled

    pooled = lax.fori_loop(0, full // 512, ffn, jnp.zeros((1, width), F32))

    for g in range(groups):
        sbuf[g : g + 1, :] = pooled[:, g * 128 : (g + 1) * 128]
    sbuf[groups:, :] = jnp.zeros((8 - groups, 128), F32)
    slot = t * n_dp + d
    pl.semaphore_wait(barrier, n_dev - 1)

    def push(k, start):
        lin = lax.rem(me + k, n_dev)
        pd, pt = lin // 2, lax.rem(lin, 2)
        c = pltpu.make_async_remote_copy(
            src_ref=sbuf, dst_ref=pool_all.at[slot], send_sem=send_sem.at[k],
            recv_sem=recv_sem.at[slot], device_id=(pd, pt), device_id_type=MESH,
        )
        if start:
            c.start()
        else:
            c.wait_send()
        return 0

    lax.fori_loop(1, n_dev, lambda k, _: push(k, True), 0)
    own_rows = pl.ds(pl.multiple_of(t * loc, loc), loc)
    oth_rows = pl.ds(pl.multiple_of(other * loc, loc), loc)
    lay_local = pltpu.make_async_copy(yb.at[own_rows], lay_o.at[t], lay_sem.at[0])
    lay_local.start()
    lay_send = pltpu.make_async_remote_copy(
        src_ref=yb.at[oth_rows], dst_ref=lay_o.at[t], send_sem=lay_sem.at[1],
        recv_sem=lay_sem.at[2], device_id=peer, device_id_type=MESH,
    )
    lay_send.start()
    pool_all[slot] = sbuf[...]

    def arrive(k, _):
        lin = lax.rem(me + k, n_dev)
        s = lax.rem(lin, 2) * n_dp + lin // 2
        pltpu.make_async_remote_copy(
            src_ref=sbuf, dst_ref=pool_all.at[s], send_sem=send_sem.at[k],
            recv_sem=recv_sem.at[s], device_id=(lin // 2, lax.rem(lin, 2)), device_id_type=MESH,
        ).wait_recv()
        return 0

    lax.fori_loop(1, n_dev, arrive, 0)

    len_col = lens_b[...][:, :1]
    units = []
    scales = []
    for v in range(2):
        raw = jnp.concatenate(
            [pool_all[v * n_dp : (v + 1) * n_dp, g, :] for g in range(groups)], axis=1
        )
        pv = raw / len_col
        scale = lax.rsqrt(jnp.sum(pv * pv, axis=1, keepdims=True) + EPSILON)
        units.append(pv * scale)
        scales.append(scale)
    u0, u1 = units
    nt = (((1,), (1,)), ((), ()))
    row_i = lax.broadcasted_iota(jnp.int32, (n_dp, n_dp), 0)
    col_i = lax.broadcasted_iota(jnp.int32, (n_dp, n_dp), 1)
    diag = row_i == col_i
    sim = lax.dot_general(u0, u1, nt, precision=HIGHEST, preferred_element_type=F32) / SOFTMAX_WARMTH
    top = jnp.max(sim, axis=1, keepdims=True)
    raw = jnp.exp(sim - top)
    total = jnp.sum(raw, axis=1, keepdims=True)
    ce = top + jnp.log(total) - jnp.sum(jnp.where(diag, sim, 0.0), axis=1, keepdims=True)
    loss = jnp.sum(ce, axis=0, keepdims=True) / n_dp
    gap = u0 - u1
    align = jnp.sum(jnp.sum(gap * gap, axis=1, keepdims=True), axis=0, keepdims=True) / n_dp
    sq = jnp.sum(u0 * u0, axis=1, keepdims=True)
    sq_row = lax.dot_general(
        jnp.ones((n_dp, width), F32), u0 * u0, nt, precision=HIGHEST, preferred_element_type=F32
    )
    inner = lax.dot_general(u0, u0, nt, precision=HIGHEST, preferred_element_type=F32)
    pot = jnp.where(diag, 0.0, jnp.exp(-2.0 * (sq + sq_row - 2.0 * inner)))
    uni = jnp.log(
        jnp.sum(jnp.sum(pot, axis=1, keepdims=True), axis=0, keepdims=True) / (n_dp * (n_dp - 1))
    )
    stat_i = lax.broadcasted_iota(jnp.int32, (8, 128), 0)
    loss_o[...] = jnp.where(stat_i == 0, loss, jnp.where(stat_i == 1, align, uni))
    d_sim = (raw / total - jnp.where(diag, 1.0, 0.0)) / SOFTMAX_WARMTH
    d_u0 = jnp.dot(d_sim, u1, precision=HIGHEST, preferred_element_type=F32)
    d_u1 = lax.dot_general(
        d_sim, u0, (((0,), (0,)), ((), ())), precision=HIGHEST, preferred_element_type=F32
    )
    first_view = t == 0
    du = jnp.where(first_view, d_u0, d_u1)
    u = jnp.where(first_view, u0, u1)
    scale = jnp.where(first_view, scales[0], scales[1])
    d_pool = (du - u * jnp.sum(u * du, axis=1, keepdims=True)) * scale / len_col
    mine = lax.broadcasted_iota(jnp.int32, (n_dp, width), 0) == d
    pool_grad = jnp.sum(jnp.where(mine, d_pool, 0.0), axis=0, keepdims=True)

    def norm_two_back(b, sums):
        rows = pl.ds(pl.multiple_of(b * 256, 256), 256)
        pos = lax.broadcasted_iota(jnp.int32, (256, width), 0) + b * 256
        dy = cotv[rows, :].astype(F32) + jnp.where(pos < length, pool_grad, 0.0)
        n = n2[rows, :]
        g = dy * gain2
        dr = (g - jnp.mean(g, axis=1, keepdims=True) - n * jnp.mean(g * n, axis=1, keepdims=True)) * rs2[rows, :1]
        dr2[rows, :] = dr
        g2[rows, :] = (dr * (mfv[rows, :].astype(F32) * INV_KEEP)).astype(BF16)
        return (
            sums[0] + jnp.sum(dy * n, axis=0, keepdims=True),
            sums[1] + jnp.sum(dy, axis=0, keepdims=True),
        )

    zero = jnp.zeros((1, width), F32)
    gg2, gs2 = lax.fori_loop(0, full // 256, norm_two_back, (zero, zero))

    def down_copy(j, s):
        return pltpu.make_async_copy(
            gch.at[s], gd_o.at[pl.ds(pl.multiple_of(j * CH, CH), CH)], ch_sem.at[s]
        )

    for j in range(n_ch):
        s = j % 2
        if j >= 2:
            down_copy(j - 2, s).wait()
        gch[s] = dot_tn(act[:, j * CH : (j + 1) * CH], g2[...]).astype(BF16)
        down_copy(j, s).start()
    for j in range(n_ch - 2, n_ch):
        down_copy(j, j % 2).wait()

    def ffn_back(b, _):
        rows = pl.ds(pl.multiple_of(b * 512, 512), 512)
        for j in range(n_ch):
            h, o = j // per_half, (j % per_half) * CH
            cols = slice(j * CH, (j + 1) * CH)
            da = dot_nt(g2[rows, :], wdv[cols, :])
            dp = (da * dg[rows, cols].astype(F32)).astype(BF16)
            dg[rows, cols] = dp
            dr2[rows, :] += dot_nt(dp, wuv[h, :, o : o + CH])
        return 0

    lax.fori_loop(0, full // 512, ffn_back, 0)

    def up_copy(j):
        h, o = j // per_half, (j % per_half) * CH
        return pltpu.make_async_copy(
            uch.at[j % 2], gu_o.at[h, :, pl.ds(o, CH)], ch_sem.at[2 + j % 2]
        )

    for j in range(n_ch):
        if j >= 2:
            up_copy(j - 2).wait()
        uch[j % 2] = dot_tn(hl[...], dg[:, j * CH : (j + 1) * CH]).astype(BF16)
        up_copy(j).start()
    for j in range(n_ch - 2, n_ch):
        up_copy(j).wait()

    def norm_one_back(b, sums):
        rows = pl.ds(pl.multiple_of(b * 256, 256), 256)
        dh = dr2[rows, :]
        n = n1[rows, :]
        g = dh * gain1
        dr = (g - jnp.mean(g, axis=1, keepdims=True) - n * jnp.mean(g * n, axis=1, keepdims=True)) * rs1[rows, :1]
        dr2[rows, :] = dr
        g2[rows, :] = (dr * (mav[rows, :].astype(F32) * INV_KEEP)).astype(BF16)
        return (
            sums[0] + jnp.sum(dh * n, axis=0, keepdims=True),
            sums[1] + jnp.sum(dh, axis=0, keepdims=True),
        )

    gg1, gs1 = lax.fori_loop(0, full // 256, norm_one_back, (zero, zero))
    save_dr = pltpu.make_async_copy(dr2, dr1_o, out_sem.at[0])
    save_dr.start()
    ng_o[...] = jnp.concatenate([gg1, gs1, gg2, gs2, zero, zero, zero, zero], axis=0)

    lane = lax.broadcasted_iota(jnp.int32, (full, 128), 1)
    seg = (
        (lax.broadcasted_iota(jnp.int32, (128, 128), 0) < 64)
        != (lax.broadcasted_iota(jnp.int32, (128, 128), 1) < 64)
    ).astype(F32).astype(BF16)

    def go_copy(g):
        rows = pl.ds(g * 128, 128)
        return pltpu.make_async_copy(x0v.at[rows], go_o.at[rows], out_sem.at[1 + g])

    def dob_copy(g):
        return pltpu.make_async_copy(
            dov.at[pl.ds(2 * g, 2)], dob_o.at[pl.ds(2 * g, 2)], out_sem.at[1 + groups + g]
        )

    for g in range(groups):
        cf = ctxv[g]
        x0v[g * 128 : (g + 1) * 128, :] = dot_tn(cf.astype(BF16), g2[...]).astype(BF16)
        go_copy(g).start()
        dc = dot_nt(g2[...], wov[g * 128 : (g + 1) * 128, :]).astype(BF16).astype(F32)
        hi, mid, lo = split_three(dc * cf)
        delta = dot_nn(hi.astype(BF16), seg) + dot_nn(mid.astype(BF16), seg) + dot_nn(lo.astype(BF16), seg)
        hi, mid, lo = split_three(delta)
        for a in range(2):
            own = (lane < 64) if a == 0 else (lane >= 64)
            first = 64 if a == 0 else 0
            extra = jnp.where(
                lane == first, hi, jnp.where(lane == first + 1, mid, jnp.where(lane == first + 2, lo, 0.0))
            )
            dov[2 * g + a] = jnp.where(own, dc, extra).astype(BF16)
        dob_copy(g).start()
    for g in range(groups):
        go_copy(g).wait()
        dob_copy(g).wait()
    save_dr.wait()
    lax.fori_loop(1, n_dev, lambda k, _: push(k, False), 0)
    lay_local.wait()
    lay_send.wait()


def middle(lengths, lens_b, vecs, ctx, x0, ma, mf, cot, wo, wu, wd, n_dp):
    full, width = x0.shape
    loc = full // 2
    groups = width // 128
    ff = wd.shape[0]
    n_dev = 2 * n_dp
    sds = jax.ShapeDtypeStruct
    anyspec = pl.BlockSpec(memory_space=pl.ANY)
    vspec = pl.BlockSpec(memory_space=pltpu.VMEM)
    outs = [
        sds((2, loc, width), BF16), sds((8, 128), F32), sds((ff, width), BF16), sds(wu.shape, BF16),
        sds((width, width), BF16), sds((8, width), F32), sds((full, width), F32),
        sds((2 * groups, full, 128), BF16),
    ]
    vm = pltpu.VMEM
    dma = pltpu.SemaphoreType.DMA
    return pl.pallas_call(
        middle_kernel,
        out_shape=outs,
        in_specs=[pl.BlockSpec(memory_space=pltpu.SMEM), vspec, vspec] + [anyspec] * 8,
        out_specs=[anyspec, vspec, anyspec, anyspec, anyspec, vspec, anyspec, anyspec],
        scratch_shapes=[
            vm(ctx.shape, F32), vm((full, width), BF16), vm((full, width), BF16),
            vm((full, width), BF16), vm((full, width), BF16), vm(wo.shape, BF16),
            vm(wu.shape, BF16), vm(wd.shape, BF16),
            vm((full, width), F32), vm((full, width), F32), vm((full, 128), F32), vm((full, 128), F32),
            vm((full, width), BF16), vm((full, ff), BF16), vm((full, ff), BF16),
            vm((full, width), BF16), vm((full, width), F32), vm((full, width), BF16),
            vm((8, 128), F32), vm((n_dev, 8, 128), F32), vm((2, CH, width), BF16),
            vm((2, width, CH), BF16), vm((2 * groups, full, 128), BF16), vm((512, width), F32),
            dma((8,)), dma((3,)), dma((n_dev,)), dma((n_dev,)), dma((4,)), dma((1 + 2 * groups,)),
        ],
        compiler_params=pltpu.CompilerParams(
            collective_id=1, has_side_effects=True, vmem_limit_bytes=VMEM_LIMIT
        ),
        name="middle",
    )(lengths, lens_b, vecs, ctx, x0, ma, mf, cot, wo, wu, wd)


def back_kernel(
    lens, qb, dob, qkv, wq, x0, dr1, d_in,
    gq_o, gt_o,
    qbv, dobv, qkvv, wqv, xv, xt, drv, dinv, dq3, acc, gch, stage, got, gtv,
    in_sem, ch_sem, send_sem,
):
    d = lax.axis_index("dp")
    t = lax.axis_index("tensor")
    other = 1 - t
    peer = (d, other)
    full, width = xv.shape
    loc = full // 2
    half_w = qkvv.shape[2]
    hw = half_w // 3
    pairs = hw // 128

    barrier = pltpu.get_barrier_semaphore()
    pl.semaphore_signal(barrier, inc=1, device_id=peer, device_id_type=MESH)
    srcs = (qb, dob, qkv, x0, wq, dr1, d_in)
    dsts = (qbv, dobv, qkvv, xv, wqv, drv, dinv)
    loads = [pltpu.make_async_copy(s, v, in_sem.at[i]) for i, (s, v) in enumerate(zip(srcs, dsts))]
    for c in loads:
        c.start()
    length = lens[d]
    lane = lax.broadcasted_iota(jnp.int32, (full, 128), 1)
    bias = jnp.where(
        lax.broadcasted_iota(jnp.int32, (full, 128), 0) < length, 0.0, MASKED_SCORE
    )
    for c in loads[:3]:
        c.wait()
    kb = 512

    def head_pair(i, _):
        h = i // pairs
        off = (i - h * pairs) * 128

        def part(c):
            return qkvv[h, :, pl.ds(pl.multiple_of(c * hw + off, 128), 128)]

        k2 = part(1)
        k2f = k2.astype(F32)
        k2t = k2f.T.astype(BF16)
        v2f = part(2).astype(F32)
        dks, dvs, dqs = [], [], []
        for a in range(2):
            own = (lane < 64) if a == 0 else (lane >= 64)
            first = 64 if a == 0 else 0
            lane3 = jnp.logical_and(lane >= first, lane < first + 3)
            minus = jnp.where(lane3, -1.0, 0.0)
            ka = jnp.where(own, k2f, jnp.where(lane == first + 3, bias, minus)).astype(BF16)
            va = jnp.where(own, v2f, minus).astype(BF16)
            qa = qbv[2 * i + a]
            da = dobv[2 * i + a]
            dk, dv = [], []
            dqt = None
            for b in range(full // kb):
                rows = slice(b * kb, (b + 1) * kb)
                p = jnp.exp(dot_nt(ka[rows], qa))
                ds = (p * dot_nt(va[rows], da)).astype(BF16)
                dv.append(dot_nn(p.astype(BF16), da))
                dk.append(dot_nn(ds, qa))
                term = dot_nn(k2t[a * 64 : (a + 1) * 64, rows], ds)
                dqt = term if dqt is None else dqt + term
            dks.append(dk)
            dvs.append(dv)
            dqs.append(dqt)
        low_half = lax.broadcasted_iota(jnp.int32, (kb, 128), 1) < 64
        for b in range(full // kb):
            rows = slice(b * kb, (b + 1) * kb)
            dq3[h, rows, pl.ds(pl.multiple_of(hw + off, 128), 128)] = jnp.where(
                low_half, dks[0][b], dks[1][b]
            ).astype(BF16)
            dq3[h, rows, pl.ds(pl.multiple_of(2 * hw + off, 128), 128)] = jnp.where(
                low_half, dvs[0][b], dvs[1][b]
            ).astype(BF16)
        dq = jnp.concatenate(dqs, axis=0) * HEAD_DIM**-0.5
        dq3[h, :, pl.ds(pl.multiple_of(off, 128), 128)] = dq.T.astype(BF16)
        return 0

    lax.fori_loop(0, 2 * pairs, head_pair, 0)
    for c in loads[3:]:
        c.wait()

    pl.semaphore_wait(barrier, 1)
    own_rows = pl.ds(pl.multiple_of(t * loc, loc), loc)
    oth_rows = pl.ds(pl.multiple_of(other * loc, loc), loc)

    def d_input(rows):
        return dot_nt(dq3[0, rows, :], wqv[0]) + dot_nt(dq3[1, rows, :], wqv[1]) + drv[rows, :]

    for s in range(loc // 256):
        stage[s * 256 : (s + 1) * 256, :] = d_input(
            pl.ds(pl.multiple_of(other * loc + s * 256, 256), 256)
        ).astype(BF16)
    send = pltpu.make_async_remote_copy(
        src_ref=stage, dst_ref=got, send_sem=send_sem.at[0], recv_sem=send_sem.at[1],
        device_id=peer, device_id_type=MESH,
    )
    send.start()
    for s in range(loc // 256):
        acc[s * 256 : (s + 1) * 256, :] = d_input(
            pl.ds(pl.multiple_of(t * loc + s * 256, 256), 256)
        )
    for c in range(width // 256):
        cols = slice(c * 256, (c + 1) * 256)
        xt[cols, :] = (xv[:, cols].astype(F32) * INV_KEEP).T.astype(BF16)

    def q_copy(j):
        h, o = j // 3, (j % 3) * hw
        return pltpu.make_async_copy(gch.at[j % 2], gq_o.at[h, :, pl.ds(o, hw)], ch_sem.at[j % 2])

    for j in range(6):
        h, o = j // 3, (j % 3) * hw
        if j >= 2:
            q_copy(j - 2).wait()
        gch[j % 2] = dot_nn(xt[...], dq3[h, :, o : o + hw]).astype(BF16)
        q_copy(j).start()
    send.wait()
    for s in range(loc // 256):
        rows = slice(s * 256, (s + 1) * 256)
        gtv[rows, :] = (
            jnp.where(dinv[t, rows, :] != 0, acc[rows, :], 0.0)
            + jnp.where(dinv[other, rows, :] != 0, got[rows, :].astype(F32), 0.0)
        ) * INV_KEEP
    out = pltpu.make_async_copy(gtv, gt_o, ch_sem.at[2])
    out.start()
    for j in range(4, 6):
        q_copy(j).wait()
    out.wait()


def back(lengths, qb, dob, qkv, wq, x0, dr1, d_in):
    full, width = x0.shape
    loc = full // 2
    half_w = qkv.shape[2]
    sds = jax.ShapeDtypeStruct
    anyspec = pl.BlockSpec(memory_space=pl.ANY)
    vm = pltpu.VMEM
    dma = pltpu.SemaphoreType.DMA
    return pl.pallas_call(
        back_kernel,
        out_shape=[sds(wq.shape, BF16), sds((loc, width), F32)],
        in_specs=[pl.BlockSpec(memory_space=pltpu.SMEM)] + [anyspec] * 7,
        out_specs=[anyspec, anyspec],
        scratch_shapes=[
            vm(qb.shape, BF16), vm(dob.shape, BF16), vm(qkv.shape, BF16), vm(wq.shape, BF16),
            vm(x0.shape, BF16), vm((width, full), BF16), vm(dr1.shape, F32), vm(d_in.shape, jnp.int32),
            vm(qkv.shape, BF16), vm((loc, width), F32), vm((2, width, half_w // 3), BF16),
            vm((loc, width), BF16), vm((loc, width), BF16), vm((loc, width), F32),
            dma((7,)), dma((3,)), dma((2,)),
        ],
        compiler_params=pltpu.CompilerParams(
            collective_id=2, has_side_effects=True, vmem_limit_bytes=VMEM_LIMIT
        ),
        name="back",
    )(lengths, qb, dob, qkv, wq, x0, dr1, d_in)


def per_device(
    tokens, lengths, drop_in, drop_attn, drop_ffn, qkv_weight, out_weight, up_weight, down_weight,
    gain_first, shift_first, gain_second, shift_second, cotangent,
):
    n_dp = lax.axis_size("dp")
    width = tokens.shape[2]
    wq = qkv_weight.reshape(width, -1)
    x0, ma, mf, cot, wqf, wof, wuf, wdf, qkv, qb, ctx = front(
        lengths, tokens[0], drop_in[0], drop_attn[0], drop_ffn[0], cotangent[0],
        wq, out_weight, up_weight, down_weight,
    )
    lens_b = jnp.broadcast_to(lengths.astype(F32)[:, None], (n_dp, 128))
    vecs = jnp.stack([gain_first, shift_first, gain_second, shift_second] * 2)
    lay, stats, gd, gu, go, ng, dr1, dob = middle(
        lengths, lens_b, vecs, ctx, x0, ma, mf, cot,
        wof.reshape(width, width), wuf, wdf.reshape(-1, width), n_dp,
    )
    gq, gt = back(lengths, qb, dob, qkv, wqf, x0, dr1, drop_in[0])
    halves = [
        gq, go.reshape(2, -1, width), gu, gd.reshape(2, -1, width),
    ]
    summed = []
    for g in halves:
        g = lax.psum_scatter(g, "tensor", scatter_dimension=0, tiled=False)
        summed.append(lax.psum(g, "dp").astype(F32))
    norms = lax.psum(ng, ("dp", "tensor"))
    return (
        lay[None], gt[None],
        summed[0].reshape(qkv_weight.shape), summed[1], summed[2], summed[3],
        norms[0], norms[1], norms[2], norms[3],
        stats[0, 0], stats[1, 0], stats[2, 0],
    )


def solution(mesh):
    act = P("dp", None, "tensor", None)
    in_specs = (
        P("dp", "tensor", None), P(), act, act, act,
        P(None, None, "tensor"), P("tensor", None), P(None, "tensor"), P("tensor", None),
        P(), P(), P(), P(), act,
    )
    out_specs = (
        act, P("dp", "tensor", None),
        P(None, None, "tensor"), P("tensor", None), P(None, "tensor"), P("tensor", None),
        P(), P(), P(), P(), P(), P(), P(),
    )
    return jax.shard_map(
        per_device, mesh=mesh, in_specs=in_specs, out_specs=out_specs, check_vma=False
    )
```

time: 1060 us -> 708 us (0.67)
  Pallas kernels: 0 us -> 371 us
  matrix products: 224 us -> 0 us
  waiting for transfers between devices: 425 us -> 242 us
  other arithmetic: 140 us -> 8.19 us
  blocking collectives: 159 us -> 42.9 us
  local copies, waits for them, and re-layouts: 81.4 us -> 22.7 us
    pallas_call x0 -> x3, Pallas kernels: none -> 371 us  [the longest x1 243 us: front(): pl.pallas_call(front_kernel, out_shape=outs, in_specs=[pl.BlockSpec(memor...]
    dot_general x43 -> x0, matrix products: 224 us -> none  [the longest x4 28.2 us: one_block(): jnp.einsum('qhd,khd->hqk', d_block, values, preferred_element_type=jnp.fl...]
    psum x1, waiting for transfers between devices: 341 us -> 192 us  [per_device(): summed.append(lax.psum(g, 'dp').astype(F32))]
    unnamed x1 -> x0, blocking collectives: 71.8 us -> none
    convert_element_type x10 -> x4, other arithmetic: 75.8 us -> 8.19 us  [the longest x3 7.53 us: per_device(): summed.append(lax.psum(g, 'dp').astype(F32))]
    all_gather x4 -> x0, waiting for transfers between devices: 48.8 us -> none  [the longest x1 14.3 us: per_device(): x_full = lax.all_gather(x_low, 'tensor', axis=2, tiled=True)]
    reduce_sum x21 -> x0, other arithmetic: 47.9 us -> none  [the longest x4 12.2 us: one_block(): row_total = jnp.sum(raw_weights, axis=-1, keepdims=True)]
    all_gather x1 -> x0, blocking collectives: 42.2 us -> none  [per_device(): lax.all_gather(pooled_part, ('dp', 'tensor'), axis=0, tiled=True)]
  transfers between devices with their start and end apart: 9 -> 5, of which waited for: 8 -> 5; matrix products, arithmetic and copies ran while one was open for 4% -> 1% of each run, Pallas kernels for 0% -> 0%
where the time goes in v1:
time: 708 us; the launch traced here: 702 us
  Pallas kernels  371 us (52%)
  waiting for transfers between devices  242 us (34%)
  blocking collectives  42.9 us (6%)
  local copies, waits for them, and re-layouts  22.7 us (3%)
  between operations  14.3 us (2%)
  other arithmetic  8.19 us (1%)
    pallas_call x1, Pallas kernels, front(): pl.pallas_call(front_kernel, out_shape=outs, in_specs=[pl.BlockSpec(memor...  243 us
    psum x1, waiting for transfers between devices, per_device(): summed.append(lax.psum(g, 'dp').astype(F32))  192 us
    pallas_call x1, Pallas kernels, middle(): pl.pallas_call(middle_kernel, out_shape=outs, in_specs=[pl.BlockSpec(memo...  79.1 us
    pallas_call x1, Pallas kernels, back(): pl.pallas_call(back_kernel, out_shape=[sds(wq.shape, BF16), sds((loc, wid...  48.9 us
    reduce_scatter x4, waiting for transfers between devices, per_device(): g = lax.psum_scatter(g, 'tensor', scatter_dimension=0, tiled=False)  48.1 us
    psum x1, blocking collectives, per_device(): norms = lax.psum(ng, ('dp', 'tensor'))  42.9 us
  transfers between devices with their start and end apart: 5, of which 5 were waited for; matrix products, arithmetic and copies ran while one was open for 1% of the time, Pallas kernels for 0%

profile of v1, /device:TPU:0, one launch (start us, length us, event | category | flops | bytes accessed | tf_op | source)
XLA Modules:
  0.0 701.7 jit_solution(3438335003578836599)
XLA Ops:
  7.9 0.7 stack.19
  10.0 0.7 stack.22
  10.6 2.6 copy.29
  13.3 2.2 copy.30.wq
  16.1 243.0 %front.1 = (bf16[1024,768]{1,0:T(8,128)(2,1)}, bf16[1024,768]{1,0:T(8,128)(2,1)}, bf16[1024,768]{1,0:T(8,128)(2,1)}, bf16[1024,768]{1,0:T(8,128)(2,1)}, bf16[2,7...) custom-call(s32[16]{0:T(128)} %lens.5, ...), custom_call_target="tpu_custom_call" | custom-call | tf_op jit(solution)/shard_map/front/pallas_call | solution.py:256
  259.8 79.1 %middle.1 = (bf16[2,512,768]{2,1,0:T(8,128)(2,1)}, f32[8,128]{1,0:T(8,128)}, bf16[3072,768]{1,0:T(8,128)(2,1)}, bf16[2,768,1536]{2,1,0:T(8,128)(2,1)}, bf16[768,...) custom-call(s32[16]{0:T(128)} %lens.5, ...), custom_call_target="tpu_custom_call" | custom-call | tf_op jit(solution)/shard_map/middle/pallas_call | solution.py:595
  338.9 48.9 %back.1 = (bf16[2,768,1152]{2,1,0:T(8,128)(2,1)}, f32[512,768]{1,0:T(8,128)}) custom-call(s32[16]{0:T(128)} %lens.5, bf16[12,1024,128]{2,1,0:T(8,128)(2,1)} %get-tuple-element.43.qb, bf16[12,1024,128]{2,1,0:T(8,128)(2,1)} %get-tuple-element.44.dob, bf16[2,1024,1152]{2,1,0:T(8,128)(2,1)} %get-tuple-element.45.qkv, ...), custom_call_target="tpu_custom_call" | custom-call | tf_op jit(solution)/shard_map/back/pallas_call | solution.py:757
  387.9 0.7 reduce-scatter.7.cloned.1.call-update
  390.0 7.5 %reduce-scatter.5.cloned.1.call-done = bf16[1,768,1152]{2,1,0:T(8,128)(2,1)} async-done(((bf16[2,768,1152]{2,1,0:T(8,128)(2,1)}), bf16[1,768,1152]{2,1,0:T(8,128)(2,1)}) %reduce-scatter.5.cloned.1.call-update) | async-done | bytes 1769488 | tf_op jit(solution)/shard_map/reduce_scatter | solution.py:799
  397.5 3.9 copy.31
  401.4 8.4 %reduce-scatter.7.cloned.1.call-done = bf16[1,384,768]{2,1,0:T(8,128)(2,1)} async-done(((bf16[2,384,768]{2,1,0:T(8,128)(2,1)}), bf16[1,384,768]{2,1,0:T(8,128)(2,1)}) %reduce-scatter.7.cloned.1.call-update) | async-done | bytes 589840 | tf_op jit(solution)/shard_map/reduce_scatter | solution.py:799
  409.8 16.1 %reduce-scatter.9.cloned.1.call-done = bf16[1,768,1536]{2,1,0:T(8,128)(2,1)} async-done(((bf16[2,768,1536]{2,1,0:T(8,128)(2,1)}), bf16[1,768,1536]{2,1,0:T(8,128)(2,1)}) %reduce-scatter.9.cloned.1.call-update) | async-done | bytes 2359312 | tf_op jit(solution)/shard_map/reduce_scatter | solution.py:799
  425.9 16.1 %reduce-scatter.11.cloned.1.call-done = bf16[1,1536,768]{2,1,0:T(8,128)(2,1)} async-done(((bf16[2,1536,768]{2,1,0:T(8,128)(2,1)}), bf16[1,1536,768]{2,1,0:T(8,128)(2,1)}) %reduce-scatter.11.cloned.1.call-update) | async-done | bytes 2359312 | tf_op jit(solution)/shard_map/reduce_scatter | solution.py:799
  442.0 0.7 copy-done.4
  442.7 42.9 %psum.39 = f32[8,768]{1,0:T(8,128)S(1)} all-reduce(f32[8,768]{1,0:T(8,128)S(1)} %copy-done.4), channel_id=1, replica_groups=mesh['dp'=16,'tensor'=2] {'dp','tensor'}, use_global_device_ids=true, to_apply=%region_8.0 | all-reduce | flops 6144 | bytes 49152 | tf_op jit(solution)/shard_map/psum | solution.py:801
  485.6 1.3 fusion
  487.5 192.4 %all-reduce.3.cloned.1.call-done = (bf16[768,3,384]{0,2,1:T(8,128)(2,1)}, bf16[384,768]{1,0:T(8,128)(2,1)}, bf16[768,1536]{1,0:T(8,128)(2,1)}, bf16[1536,768]{1,0:T(8,128)(2,1)}) async-done(((bf16[768,3,384]{0,2,1:T(8,128)(2,1)}, bf16[384,768]{1,0:T(8,128)(2,1)}, bf16[768,1536]{1,0:T(8,128)(2,1)}, bf16[1536,768]{1,0:T(8,128)(2,1)}), (bf16[768,3,384]{0,2,1:T(8,128)(2,1)}, bf16[384,768]{1,0:T(8,128)(2,1)}, ...) | async-done | bytes 7077904 | tf_op jit(solution)/shard_map/psum | solution.py:800
  679.9 2.2 convert_element_type.14
  682.1 4.2 copy.32
  686.3 2.8 convert_element_type.15
  689.1 2.5 convert_element_type.16
  691.7 1.1 copy.39
  692.8 0.8 copy-done.3
  693.6 1.1 copy.40
  (23 shorter events, 5.4 us)
Async XLA Ops:
  7.2 390.4 %reduce-scatter.5.cloned.1.call-start = ((), (), s32[]{:S(2)}) async-start(), calls=%async_computation.4 | async-start | bytes 5308416 | tf_op jit(solution)/shard_map/reduce_scatter | solution.py:799
  387.9 21.9 %reduce-scatter.7.cloned.1.call-start = ((), (), s32[]{:S(2)}) async-start(), calls=%async_computation.5 | async-start | bytes 1769472 | tf_op jit(solution)/shard_map/reduce_scatter | solution.py:799
  388.7 37.2 %reduce-scatter.9.cloned.1.call-start = ((), (), s32[]{:S(2)}) async-start(), calls=%async_computation.6 | async-start | bytes 7077888 | tf_op jit(solution)/shard_map/reduce_scatter | solution.py:799
  389.4 52.6 %reduce-scatter.11.cloned.1.call-start = ((), (), s32[]{:S(2)}) async-start(), calls=%async_computation.7 | async-start | bytes 7077888 | tf_op jit(solution)/shard_map/reduce_scatter | solution.py:799
  390.0 290.0 %all-reduce.3.cloned.1.call-start = ((), (), s32[]{:S(2)}) async-start(), calls=%async_computation.8 | async-start | bytes 14155776 | tf_op jit(solution)/shard_map/psum | solution.py:800
  442.0 0.7 copy-start.4
  682.1 4.2 copy-start.1
  686.3 2.8 copy-start
  689.1 2.6 copy-start.2
  691.6 2.0 copy-start.3
Sparse Core Ops, SparseCore 0:
  388.0 9.4 reduce-scatter.4
  399.9 9.8 reduce-scatter.6
  412.1 13.7 reduce-scatter.8
  428.2 13.7 reduce-scatter.10
  448.8 231.0 all-reduce.2

commit v2 on v1

v2 whole, which is shorter than its diff:
```python
import functools
import math

import jax
import jax.numpy as jnp
from jax import lax
from jax.experimental import pallas as pl
from jax.experimental.pallas import tpu as pltpu
from jax.sharding import PartitionSpec as P

HEAD_DIM = 64
INV_KEEP = 1.0 / 0.9
SOFTMAX_WARMTH = 0.05
EPSILON = 1e-06
MASKED_SCORE = -1e30
MESH = pl.DeviceIdType.MESH
F32 = jnp.float32
BF16 = jnp.bfloat16
VMEM_LIMIT = 60 * 2**20
HIGHEST = lax.Precision.HIGHEST

TAIL_P = 0.3
TAIL = (
    0.11962929778234735,
    0.12075397394392673,
    0.09991336806236217,
    0.1285620774207718,
    -0.05368457414666341,
    0.20635459819946347,
    -0.15720376083821283,
    0.03567494667807555,
)


def dot_nn(a, b):
    return jnp.dot(a, b, preferred_element_type=F32)


def dot_nt(a, b):
    return lax.dot_general(a, b, (((1,), (1,)), ((), ())), preferred_element_type=F32)


def dot_tn(a, b):
    return lax.dot_general(a, b, (((0,), (0,)), ((), ())), preferred_element_type=F32)


def gelu_pair(x):
    z = jnp.abs(x)
    bell = jnp.exp(x * x * -0.5)
    t = 1.0 / (1.0 + TAIL_P * z)
    acc = jnp.full_like(t, TAIL[-1])
    for c in TAIL[-2::-1]:
        acc = acc * t + c
    tail = acc * t * bell
    cdf = jnp.where(x < 0.0, tail, 1.0 - tail)
    return x * cdf, cdf + x * (bell * (1.0 / math.sqrt(2.0 * math.pi)))


def split_three(v):
    hi = v.astype(BF16).astype(F32)
    rest = v - hi
    mid = rest.astype(BF16).astype(F32)
    return hi, mid, rest - mid


def front_kernel(
    lens, tok, d_in, d_at, d_ff, cot, wq, wo, wu, wd,
    x0_o, ma_o, mf_o, cot_o, wq_o, wo_o, wu_o, wd_o, qkv_o, qb_o, ctx_o,
    xv, xl, wv, qs, ms, tokv, st, qbv, ctxv, in_sem, loc_sem, send_sem, recv_sem, out_sem,
):
    d = lax.axis_index("dp")
    t = lax.axis_index("tensor")
    other = 1 - t
    peer = (d, other)
    loc = tok.shape[0]
    full = 2 * loc
    half_w = wq.shape[1]
    hw = half_w // 3
    pairs = hw // 128

    barrier = pltpu.get_barrier_semaphore()
    pl.semaphore_signal(barrier, inc=1, device_id=peer, device_id_type=MESH)

    loads = [
        pltpu.make_async_copy(tok, tokv, in_sem.at[0]),
        pltpu.make_async_copy(d_in, ms.at[0], in_sem.at[1]),
        pltpu.make_async_copy(wq, wv.at[t], in_sem.at[2]),
        pltpu.make_async_copy(d_at, ms.at[1], in_sem.at[3]),
        pltpu.make_async_copy(d_ff, ms.at[2], in_sem.at[4]),
    ]
    for c in loads:
        c.start()
    own_rows = pl.ds(pl.multiple_of(t * loc, loc), loc)

    def remote(i, src, dst):
        return pltpu.make_async_remote_copy(
            src_ref=src, dst_ref=dst, send_sem=send_sem.at[i], recv_sem=recv_sem.at[i],
            device_id=peer, device_id_type=MESH,
        )

    pl.semaphore_wait(barrier, 1)
    send_wq = remote(0, wq, wv.at[t])
    send_wq.start()
    loads[0].wait()
    loads[1].wait()
    st[0] = jnp.where(ms[0, other] != 0, tokv[...].astype(F32), 0.0).astype(BF16)
    send_x = remote(1, st.at[0], xv.at[own_rows])
    send_x.start()
    own_x = jnp.where(ms[0, t] != 0, tokv[...].astype(F32), 0.0)
    xv[own_rows, :] = own_x.astype(BF16)
    xl[own_rows, :] = (own_x * INV_KEEP).astype(BF16)
    loads[3].wait()
    st[1] = ms[1, other].astype(F32).astype(BF16)
    st[2] = ms[1, t].astype(F32).astype(BF16)
    loads[4].wait()
    st[3] = ms[2, other].astype(F32).astype(BF16)
    st[4] = ms[2, t].astype(F32).astype(BF16)
    sends = [
        remote(2, wo, wo_o),
        remote(3, st.at[1], ma_o.at[own_rows]),
        remote(4, wu, wu_o),
        remote(5, wd, wd_o),
        remote(6, st.at[3], mf_o.at[own_rows]),
        remote(7, cot.at[other], cot_o),
    ]
    for c in sends:
        c.start()
    more = [
        pltpu.make_async_copy(st.at[2], ma_o.at[own_rows], loc_sem.at[0]),
        pltpu.make_async_copy(st.at[4], mf_o.at[own_rows], loc_sem.at[1]),
    ]
    for c in more:
        c.start()

    loads[2].wait()
    send_wq.wait_recv()
    send_x.wait_recv()
    oth_rows = pl.ds(pl.multiple_of(other * loc, loc), loc)
    xl[oth_rows, :] = (xv[oth_rows, :].astype(F32) * INV_KEEP).astype(BF16)
    save_x = pltpu.make_async_copy(xv, x0_o, loc_sem.at[2])
    save_x.start()
    save_w = pltpu.make_async_copy(wv, wq_o, loc_sem.at[3])
    save_w.start()

    for h in range(2):
        for c in range(3):
            def project(b, _, h=h, c=c):
                rows = pl.ds(pl.multiple_of(b * 512, 512), 512)
                qs[h, rows, c * hw : (c + 1) * hw] = dot_nn(
                    xl[rows, :], wv[h, :, c * hw : (c + 1) * hw]
                ).astype(BF16)
                return 0

            lax.fori_loop(0, full // 512, project, 0)
    save_qkv = pltpu.make_async_copy(qs, qkv_o, loc_sem.at[4])
    save_qkv.start()

    length = lens[d]
    bias = jnp.where(
        lax.broadcasted_iota(jnp.int32, (full, 128), 0) < length, 0.0, MASKED_SCORE
    )
    lane = lax.broadcasted_iota(jnp.int32, (full, 128), 1)
    lane_q = lax.broadcasted_iota(jnp.int32, (512, 128), 1)

    def out_copies(i):
        return [
            pltpu.make_async_copy(qbv.at[pl.ds(2 * i, 2)], qb_o.at[pl.ds(2 * i, 2)], out_sem.at[0, i]),
            pltpu.make_async_copy(ctxv.at[i], ctx_o.at[i], out_sem.at[1, i]),
        ]

    def head_pair(i, _):
        h = i // pairs
        off = (i - h * pairs) * 128

        def part(c):
            return qs[h, :, pl.ds(pl.multiple_of(c * hw + off, 128), 128)].astype(F32)

        q2 = part(0) * HEAD_DIM**-0.5
        k2 = part(1)
        v2 = part(2)
        keys, vals, ques = [], [], []
        for a in range(2):
            own = (lane < 64) if a == 0 else (lane >= 64)
            first = 64 if a == 0 else 0
            keys.append(jnp.where(own, k2, jnp.where(lane == first, bias, 0.0)).astype(BF16))
            ques.append(jnp.where(own, q2, jnp.where(lane == first, 1.0, 0.0)).astype(BF16))
            vals.append(jnp.where(own, v2, 1.0).astype(BF16))
        for b in range(full // 512):
            rows = slice(b * 512, (b + 1) * 512)
            tops, outs = [], []
            for a in range(2):
                s = dot_nt(ques[a][rows], keys[a])
                top = jnp.max(s, axis=1, keepdims=True)
                p = jnp.exp(s - top).astype(BF16)
                outs.append(dot_nn(p, vals[a]))
                tops.append(top)
            low_half = lane_q < 64
            num = jnp.where(low_half, outs[0], outs[1])
            den = pltpu.roll(jnp.where(low_half, outs[1], outs[0]), 64, 1)
            ctxv[i, rows, :] = num / den
            for a in range(2):
                hi, mid, lo = split_three(tops[a] + jnp.log(outs[a]))
                own = low_half if a == 0 else jnp.logical_not(low_half)
                first = 64 if a == 0 else 0
                extra = jnp.where(
                    lane_q == first, hi,
                    jnp.where(lane_q == first + 1, mid,
                              jnp.where(lane_q == first + 2, lo,
                                        jnp.where(lane_q == first + 3, 1.0, 0.0))),
                )
                qbv[2 * i + a, rows, :] = jnp.where(own, q2[rows], extra).astype(BF16)
        for c in out_copies(i):
            c.start()
        return 0

    lax.fori_loop(0, 2 * pairs, head_pair, 0)

    def drain(i, _):
        for c in out_copies(i):
            c.wait()
        return 0

    lax.fori_loop(0, 2 * pairs, drain, 0)
    send_wq.wait_send()
    send_x.wait_send()
    for c in sends:
        c.wait()
    for c in more + [save_x, save_w, save_qkv]:
        c.wait()


def front(lengths, tok, d_in, d_at, d_ff, cot, wq, wo, wu, wd):
    loc, width = tok.shape
    full = 2 * loc
    half_w = wq.shape[1]
    groups = width // 128
    sds = jax.ShapeDtypeStruct
    anyspec = pl.BlockSpec(memory_space=pl.ANY)
    outs = [
        sds((full, width), BF16), sds((full, width), BF16), sds((full, width), BF16),
        sds((loc, width), BF16),
        sds((2,) + wq.shape, BF16), sds(wo.shape, BF16), sds(wu.shape, BF16), sds(wd.shape, BF16),
        sds((2, full, half_w), BF16), sds((2 * groups, full, 128), BF16),
        sds((groups, full, 128), F32),
    ]
    return pl.pallas_call(
        front_kernel,
        out_shape=outs,
        in_specs=[pl.BlockSpec(memory_space=pltpu.SMEM)] + [anyspec] * 9,
        out_specs=[anyspec] * len(outs),
        scratch_shapes=[
            pltpu.VMEM((full, width), BF16), pltpu.VMEM((full, width), BF16),
            pltpu.VMEM((2,) + wq.shape, BF16), pltpu.VMEM((2, full, half_w), BF16),
            pltpu.VMEM((3, 2, loc, width), jnp.int32), pltpu.VMEM((loc, width), BF16),
            pltpu.VMEM((5, loc, width), BF16),
            pltpu.VMEM((2 * groups, full, 128), BF16), pltpu.VMEM((groups, full, 128), F32),
            pltpu.SemaphoreType.DMA((5,)), pltpu.SemaphoreType.DMA((5,)),
            pltpu.SemaphoreType.DMA((8,)), pltpu.SemaphoreType.DMA((8,)),
            pltpu.SemaphoreType.DMA((2, groups)),
        ],
        compiler_params=pltpu.CompilerParams(
            collective_id=0, has_side_effects=True, vmem_limit_bytes=VMEM_LIMIT
        ),
        name="front",
    )(lengths, tok, d_in, d_at, d_ff, cot, wq, wo, wu, wd)


CH = 512


def middle_kernel(
    lens, lens_b, vecs, ctx, x0, ma, mf, cot, cot_p, wo, wo_p, wu, wu_p, wd, wd_p,
    lay_o, loss_o, act_o, dg_o, hl_o, n1_o, rs1_o, g2_o, dr2_o, ng_o,
    ctxv, x0v, mav, mfv, cotv, wov, wuv, wdv,
    n1, n2, rs1, rs2, hl, act, dg, g2, dr2, yb, sbuf, pool_all, facc,
    in_sem, lay_sem, send_sem, recv_sem, row_sem, out_sem,
):
    d = lax.axis_index("dp")
    t = lax.axis_index("tensor")
    other = 1 - t
    peer = (d, other)
    n_dp = lax.axis_size("dp")
    n_dev = 2 * n_dp
    full, width = x0v.shape
    loc = full // 2
    groups = width // 128
    ff_half = wuv.shape[2]
    n_ch = 2 * ff_half // CH
    per_half = ff_half // CH
    me = d * 2 + t

    barrier = pltpu.get_barrier_semaphore()

    def greet(k, _):
        lin = lax.rem(me + k, n_dev)
        pl.semaphore_signal(
            barrier, inc=1, device_id=(lin // 2, lax.rem(lin, 2)), device_id_type=MESH
        )
        return 0

    lax.fori_loop(1, n_dev, greet, 0)

    own_rows = pl.ds(pl.multiple_of(t * loc, loc), loc)
    oth_rows = pl.ds(pl.multiple_of(other * loc, loc), loc)
    srcs = (ctx, wo, wo_p, x0, ma, wu, wu_p, wd, wd_p, mf, cot.at[t], cot_p)
    dsts = (
        ctxv, wov.at[t], wov.at[other], x0v, mav, wuv.at[t], wuv.at[other], wdv.at[t],
        wdv.at[other], mfv, cotv.at[own_rows], cotv.at[oth_rows],
    )
    loads = [pltpu.make_async_copy(s, v, in_sem.at[i]) for i, (s, v) in enumerate(zip(srcs, dsts))]
    for c in loads:
        c.start()
    gain1, shift1, gain2, shift2 = (vecs[i : i + 1, :] for i in range(4))
    length = lens[d]

    for c in loads[:5]:
        c.wait()

    def norm_one(b, _):
        rows = pl.ds(pl.multiple_of(b * 256, 256), 256)
        c2 = jnp.concatenate([ctxv[g, rows, :].astype(BF16) for g in range(groups)], axis=1)
        branch = dot_nn(c2, wov[...].reshape(width, width))
        r = (x0v[rows, :].astype(F32) + branch * mav[rows, :].astype(F32)) * INV_KEEP
        cen = r - jnp.mean(r, axis=1, keepdims=True)
        rstd = lax.rsqrt(jnp.mean(cen * cen, axis=1, keepdims=True) + EPSILON)
        n = cen * rstd
        n1[rows, :] = n
        rs1[rows, :] = jnp.broadcast_to(rstd, (256, 128))
        hl[rows, :] = (n * gain1 + shift1).astype(BF16)
        return 0

    lax.fori_loop(0, full // 256, norm_one, 0)
    saves = [
        pltpu.make_async_copy(s, o, out_sem.at[i])
        for i, (s, o) in enumerate(((hl, hl_o), (n1, n1_o), (rs1, rs1_o)))
    ]
    for c in saves:
        c.start()
    for c in loads[5:]:
        c.wait()

    def row_copies(b):
        rows = pl.ds(pl.multiple_of(b * 512, 512), 512)
        return [
            pltpu.make_async_copy(act.at[rows], act_o.at[rows], row_sem.at[b, 0]),
            pltpu.make_async_copy(dg.at[rows], dg_o.at[rows], row_sem.at[b, 1]),
        ]

    def ffn(b, pooled):
        rows = pl.ds(pl.multiple_of(b * 512, 512), 512)
        for j in range(n_ch):
            h, o = j // per_half, (j % per_half) * CH
            pre = dot_nn(hl[rows, :], wuv[h, :, o : o + CH])
            a, da = gelu_pair(pre)
            ab = a.astype(BF16)
            act[rows, j * CH : (j + 1) * CH] = ab
            dg[rows, j * CH : (j + 1) * CH] = da.astype(BF16)
            term = dot_nn(ab, wdv[h, o : o + CH, :])
            if j == 0:
                facc[...] = term
            else:
                facc[...] += term
        for c in row_copies(b):
            c.start()
        for s in range(2):
            sub = pl.ds(pl.multiple_of(b * 512 + s * 256, 256), 256)
            r = n1[sub, :] * gain1 + shift1 + facc[s * 256 : (s + 1) * 256, :] * (
                mfv[sub, :].astype(F32) * INV_KEEP
            )
            cen = r - jnp.mean(r, axis=1, keepdims=True)
            rstd = lax.rsqrt(jnp.mean(cen * cen, axis=1, keepdims=True) + EPSILON)
            n = cen * rstd
            n2[sub, :] = n
            rs2[sub, :] = jnp.broadcast_to(rstd, (256, 128))
            y = n * gain2 + shift2
            yb[sub, :] = y.astype(BF16)
            pos = lax.broadcasted_iota(jnp.int32, (256, width), 0) + (b * 512 + s * 256)
            pooled = pooled + jnp.sum(jnp.where(pos < length, y, 0.0), axis=0, keepdims=True)
        return pooled

    pooled = lax.fori_loop(0, full // 512, ffn, jnp.zeros((1, width), F32))

    for g in range(groups):
        sbuf[g : g + 1, :] = pooled[:, g * 128 : (g + 1) * 128]
    sbuf[groups:, :] = jnp.zeros((8 - groups, 128), F32)
    slot = t * n_dp + d
    pl.semaphore_wait(barrier, n_dev - 1)

    def push(k, start):
        lin = lax.rem(me + k, n_dev)
        pd, pt = lin // 2, lax.rem(lin, 2)
        c = pltpu.make_async_remote_copy(
            src_ref=sbuf, dst_ref=pool_all.at[slot], send_sem=send_sem.at[k],
            recv_sem=recv_sem.at[slot], device_id=(pd, pt), device_id_type=MESH,
        )
        if start:
            c.start()
        else:
            c.wait_send()
        return 0

    lax.fori_loop(1, n_dev, lambda k, _: push(k, True), 0)
    lay_local = pltpu.make_async_copy(yb.at[own_rows], lay_o.at[t], lay_sem.at[0])
    lay_local.start()
    lay_send = pltpu.make_async_remote_copy(
        src_ref=yb.at[oth_rows], dst_ref=lay_o.at[t], send_sem=lay_sem.at[1],
        recv_sem=lay_sem.at[2], device_id=peer, device_id_type=MESH,
    )
    lay_send.start()
    pool_all[slot] = sbuf[...]

    def arrive(k, _):
        lin = lax.rem(me + k, n_dev)
        s = lax.rem(lin, 2) * n_dp + lin // 2
        pltpu.make_async_remote_copy(
            src_ref=sbuf, dst_ref=pool_all.at[s], send_sem=send_sem.at[k],
            recv_sem=recv_sem.at[s], device_id=(lin // 2, lax.rem(lin, 2)), device_id_type=MESH,
        ).wait_recv()
        return 0

    lax.fori_loop(1, n_dev, arrive, 0)

    len_col = lens_b[...][:, :1]
    units = []
    scales = []
    for v in range(2):
        raw = jnp.concatenate(
            [pool_all[v * n_dp : (v + 1) * n_dp, g, :] for g in range(groups)], axis=1
        )
        pv = raw / len_col
        scale = lax.rsqrt(jnp.sum(pv * pv, axis=1, keepdims=True) + EPSILON)
        units.append(pv * scale)
        scales.append(scale)
    u0, u1 = units
    nt = (((1,), (1,)), ((), ()))
    row_i = lax.broadcasted_iota(jnp.int32, (n_dp, n_dp), 0)
    col_i = lax.broadcasted_iota(jnp.int32, (n_dp, n_dp), 1)
    diag = row_i == col_i
    sim = lax.dot_general(u0, u1, nt, precision=HIGHEST, preferred_element_type=F32) / SOFTMAX_WARMTH
    top = jnp.max(sim, axis=1, keepdims=True)
    raw = jnp.exp(sim - top)
    total = jnp.sum(raw, axis=1, keepdims=True)
    ce = top + jnp.log(total) - jnp.sum(jnp.where(diag, sim, 0.0), axis=1, keepdims=True)
    loss = jnp.sum(ce, axis=0, keepdims=True) / n_dp
    gap = u0 - u1
    align = jnp.sum(jnp.sum(gap * gap, axis=1, keepdims=True), axis=0, keepdims=True) / n_dp
    sq = jnp.sum(u0 * u0, axis=1, keepdims=True)
    sq_row = lax.dot_general(
        jnp.ones((n_dp, width), F32), u0 * u0, nt, precision=HIGHEST, preferred_element_type=F32
    )
    inner = lax.dot_general(u0, u0, nt, precision=HIGHEST, preferred_element_type=F32)
    pot = jnp.where(diag, 0.0, jnp.exp(-2.0 * (sq + sq_row - 2.0 * inner)))
    uni = jnp.log(
        jnp.sum(jnp.sum(pot, axis=1, keepdims=True), axis=0, keepdims=True) / (n_dp * (n_dp - 1))
    )
    stat_i = lax.broadcasted_iota(jnp.int32, (8, 128), 0)
    loss_o[...] = jnp.where(stat_i == 0, loss, jnp.where(stat_i == 1, align, uni))
    d_sim = (raw / total - jnp.where(diag, 1.0, 0.0)) / SOFTMAX_WARMTH
    d_u0 = jnp.dot(d_sim, u1, precision=HIGHEST, preferred_element_type=F32)
    d_u1 = lax.dot_general(
        d_sim, u0, (((0,), (0,)), ((), ())), precision=HIGHEST, preferred_element_type=F32
    )
    first_view = t == 0
    du = jnp.where(first_view, d_u0, d_u1)
    u = jnp.where(first_view, u0, u1)
    scale = jnp.where(first_view, scales[0], scales[1])
    d_pool = (du - u * jnp.sum(u * du, axis=1, keepdims=True)) * scale / len_col
    mine = lax.broadcasted_iota(jnp.int32, (n_dp, width), 0) == d
    pool_grad = jnp.sum(jnp.where(mine, d_pool, 0.0), axis=0, keepdims=True)

    def norm_two_back(b, sums):
        rows = pl.ds(pl.multiple_of(b * 256, 256), 256)
        pos = lax.broadcasted_iota(jnp.int32, (256, width), 0) + b * 256
        dy = cotv[rows, :].astype(F32) + jnp.where(pos < length, pool_grad, 0.0)
        n = n2[rows, :]
        g = dy * gain2
        dr = (g - jnp.mean(g, axis=1, keepdims=True) - n * jnp.mean(g * n, axis=1, keepdims=True)) * rs2[rows, :1]
        dr2[rows, :] = dr
        g2[rows, :] = (dr * (mfv[rows, :].astype(F32) * INV_KEEP)).astype(BF16)
        return (
            sums[0] + jnp.sum(dy * n, axis=0, keepdims=True),
            sums[1] + jnp.sum(dy, axis=0, keepdims=True),
        )

    zero = jnp.zeros((1, width), F32)
    gg2, gs2 = lax.fori_loop(0, full // 256, norm_two_back, (zero, zero))

    ng_o[...] = jnp.concatenate([gg2, gs2, zero, zero, zero, zero, zero, zero], axis=0)
    more = [
        pltpu.make_async_copy(g2, g2_o, out_sem.at[3]),
        pltpu.make_async_copy(dr2, dr2_o, out_sem.at[4]),
    ]
    for c in more:
        c.start()
    for b in range(full // 512):
        for c in row_copies(b):
            c.wait()
    lax.fori_loop(1, n_dev, lambda k, _: push(k, False), 0)
    lay_local.wait()
    lay_send.wait()
    for c in saves + more:
        c.wait()


def middle(lengths, lens_b, vecs, ctx, x0, ma, mf, cot, cot_p, wo, wo_p, wu, wu_p, wd, wd_p, n_dp):
    full, width = x0.shape
    loc = full // 2
    ff = 2 * wd.shape[0]
    n_dev = 2 * n_dp
    sds = jax.ShapeDtypeStruct
    anyspec = pl.BlockSpec(memory_space=pl.ANY)
    vspec = pl.BlockSpec(memory_space=pltpu.VMEM)
    outs = [
        sds((2, loc, width), BF16), sds((8, 128), F32), sds((full, ff), BF16), sds((full, ff), BF16),
        sds((full, width), BF16), sds((full, width), F32), sds((full, 128), F32),
        sds((full, width), BF16), sds((full, width), F32), sds((8, width), F32),
    ]
    vm = pltpu.VMEM
    dma = pltpu.SemaphoreType.DMA
    return pl.pallas_call(
        middle_kernel,
        out_shape=outs,
        in_specs=[pl.BlockSpec(memory_space=pltpu.SMEM), vspec, vspec] + [anyspec] * 12,
        out_specs=[anyspec, vspec] + [anyspec] * 7 + [vspec],
        scratch_shapes=[
            vm(ctx.shape, F32), vm((full, width), BF16), vm((full, width), BF16),
            vm((full, width), BF16), vm((full, width), BF16), vm((2,) + wo.shape, BF16),
            vm((2,) + wu.shape, BF16), vm((2,) + wd.shape, BF16),
            vm((full, width), F32), vm((full, width), F32), vm((full, 128), F32), vm((full, 128), F32),
            vm((full, width), BF16), vm((full, ff), BF16), vm((full, ff), BF16),
            vm((full, width), BF16), vm((full, width), F32), vm((full, width), BF16),
            vm((8, 128), F32), vm((n_dev, 8, 128), F32), vm((512, width), F32),
            dma((12,)), dma((3,)), dma((n_dev,)), dma((n_dev,)), dma((full // 512, 2)), dma((5,)),
        ],
        compiler_params=pltpu.CompilerParams(
            collective_id=1, has_side_effects=True, vmem_limit_bytes=VMEM_LIMIT
        ),
        name="middle",
    )(lengths, lens_b, vecs, ctx, x0, ma, mf, cot, cot_p, wo, wo_p, wu, wu_p, wd, wd_p)


def sum_orders(n_dp):
    bits = n_dp.bit_length() - 1
    if bits == 4:
        return {"xy": ((0, 1, 2, 3), (1, 0, 2, 3)), "z": ((2, 3, 0, 1), (2, 3, 1, 0))}
    plain = tuple(range(bits))

    def turn(k):
        return plain[k % bits :] + plain[: k % bits] if bits else plain

    return {"xy": (turn(0), turn(2)), "z": (turn(4), turn(3))}


def back_kernel(
    lens, vecs, ng2, g2_i, dr2_i, act_i, dg_i, hl_i, n1_i, rs1_i, ctx_i, ma_i, wo, wo_p, wu, wu_p,
    wd, wd_p, qb_i, qkv_i, x0_i, wq_i, din_i,
    gq_o, go_o, gu_o, gd_o, gt_o, ng_o,
    mine, core_in, ring_in, stage, g2, dr, dobv, gin, gout, nsend, nall,
    in_sem, core_send, core_recv, ring_send, ring_recv, out_sem, nsend_sem, nrecv_sem, gt_sem,
):
    d = lax.axis_index("dp")
    t = lax.axis_index("tensor")
    other = 1 - t
    peer = (d, other)
    n_dp = lax.axis_size("dp")
    n_dev = 2 * n_dp
    me = d * 2 + t
    full, width = g2.shape
    loc = full // 2
    ff_half = wu.shape[1]
    half_w = qkv_i.shape[2]
    hw = half_w // 3
    pairs = hw // 128
    groups = width // 128
    n_cols = ff_half // CH
    rows_c = mine.shape[1]
    bits = n_dp.bit_length() - 1
    orders = sum_orders(n_dp)
    n_chunks = mine.shape[0]
    kinds = ["xy"] * n_chunks
    kinds[1] = kinds[4] = "z"

    barrier = pltpu.get_barrier_semaphore()

    def greet(k, _):
        lin = lax.rem(me + k, n_dev)
        pl.semaphore_signal(
            barrier, inc=1, device_id=(lin // 2, lax.rem(lin, 2)), device_id_type=MESH
        )
        return 0

    lax.fori_loop(1, n_dev, greet, 0)

    def load(pairs_of, first):
        copies = [
            pltpu.make_async_copy(s, v, in_sem.at[first + i]) for i, (s, v) in enumerate(pairs_of)
        ]
        for c in copies:
            c.start()
        return copies

    def core_copy(c):
        return pltpu.make_async_remote_copy(
            src_ref=stage.at[c % 3], dst_ref=core_in.at[c], send_sem=core_send.at[c],
            recv_sem=core_recv.at[c], device_id=peer, device_id_type=MESH,
        )

    def plan(c):
        steps = []
        off = 0
        size = rows_c
        place = 0
        o0, o1 = orders[kinds[c]]
        for b0, b1 in zip(o0, o1):
            size //= 2
            beta = lax.rem(d // 2**b0, 2) * other + lax.rem(d // 2**b1, 2) * t
            hop = 2**b0 * other + 2**b1 * t
            partner = d + (1 - 2 * beta) * hop
            keep = pl.multiple_of(off + beta * size, 16)
            sent = pl.multiple_of(off + (1 - beta) * size, 16)
            steps.append((partner, keep, sent, size, place))
            off = off + beta * size
            place += size
        return steps

    def ring_copy(c, s):
        if s < bits:
            partner, keep, sent, size, place = plan(c)[s]
            src, dst = mine.at[c, pl.ds(sent, size)], ring_in.at[c, pl.ds(place, size)]
        else:
            partner, keep, sent, size, place = plan(c)[2 * bits - 1 - s]
            src, dst = core_in.at[c, pl.ds(keep, size)], core_in.at[c, pl.ds(keep, size)]
        return pltpu.make_async_remote_copy(
            src_ref=src, dst_ref=dst, send_sem=ring_send.at[c, s], recv_sem=ring_recv.at[c, s],
            device_id=(partner, t), device_id_type=MESH,
        )

    def add_in(c, dst, dst_off, size, src, src_off):
        step = math.gcd(size, 384)

        def body(i, _):
            a = pl.ds(pl.multiple_of(dst_off + i * step, 16), step)
            b = pl.ds(pl.multiple_of(src_off + i * step, 16), step)
            dst[c, a, :] = (mine[c, a, :].astype(F32) + src[c, b, :].astype(F32)).astype(BF16)
            return 0

        lax.fori_loop(0, size // step, body, 0)

    def out_copies(c):
        dst = []
        if c < n_cols:
            for g in range(groups):
                dst.append((g * CH, CH, gd_o.at[pl.ds(c * CH, CH), pl.ds(g * 128, 128)]))
        elif c < 2 * n_cols:
            for g in range(CH // 128):
                col = (c - n_cols) * CH + g * 128
                dst.append((g * width, width, gu_o.at[:, pl.ds(col, 128)]))
        else:
            j = c - 2 * n_cols
            for g in range(3):
                dst.append((g * width, width, gq_o.at[:, pl.ds(g * hw + j * 128, 128)]))
            for g in range(groups):
                dst.append(
                    (3 * width + g * 128, 128, go_o.at[pl.ds(j * 128, 128), pl.ds(g * 128, 128)])
                )
        return [
            pltpu.make_async_copy(core_in.at[c, pl.ds(o, n)], r, out_sem.at[c, i])
            for i, (o, n, r) in enumerate(dst)
        ]

    last = 2 * bits + 1
    begun = {}
    now = [0]

    def advance(c, a):
        if a == 0:
            core_copy(c).wait()
            add_in(c, mine, 0, rows_c, core_in, 0)
        else:
            ring_copy(c, a - 1).wait()
            if a <= bits:
                _, keep, _, size, place = plan(c)[a - 1]
                add_in(c, core_in if a == bits else mine, keep, size, ring_in, place)
        if a < 2 * bits:
            ring_copy(c, a).start()
        else:
            for cp in out_copies(c):
                cp.start()

    def tick():
        now[0] += 1
        for c in sorted(begun):
            a = begun[c]
            if a <= 2 * bits:
                advance(c, a)
                begun[c] = a + 1

    def begin(c):
        core_copy(c).start()

    def put(ref, at, val):
        n = val.shape[0]
        for g in range(val.shape[1] // 128):
            ref[at + g * n : at + (g + 1) * n, :] = val[:, g * 128 : (g + 1) * 128].astype(BF16)

    gain1 = vecs[0:1, :]
    met = [False]

    def meet():
        if not met[0]:
            pl.semaphore_wait(barrier, n_dev - 1)
            met[0] = True

    def feed_forward(act, dg, hl, hlt, wuv, wdv):
        first = load(
            [(g2_i, g2), (act_i, act), (dr2_i, dr), (hl_i, hl), (dg_i, dg), (wd, wdv.at[t]),
             (wd_p, wdv.at[other]), (wu, wuv.at[t]), (wu_p, wuv.at[other])], 0,
        )
        first[0].wait()
        first[1].wait()
        for c in range(n_cols):
            for h, ref in ((other, stage.at[c % 3]), (t, mine.at[c])):
                col = pl.ds(pl.multiple_of(h * ff_half + c * CH, CH), CH)
                put(ref, 0, dot_tn(act[:, col], g2[...]))
                if ref is not None and h is other:
                    meet()
                    begin(c)
            tick()
            begun[c] = 0
        for cp in first[2:]:
            cp.wait()
        for k in range(groups):
            cols = slice(k * 128, (k + 1) * 128)
            hlt[cols, :] = hl[:, cols].astype(F32).T.astype(BF16)
        for k in range(n_cols):
            c = n_cols + k
            for h, ref in ((other, stage.at[c % 3]), (t, mine.at[c])):
                col = pl.ds(pl.multiple_of(h * ff_half + k * CH, CH), CH)
                for b in range(full // 512):
                    rows = slice(b * 512, (b + 1) * 512)
                    da = dot_nt(g2[rows, :], wdv[h, k * CH : (k + 1) * CH, :])
                    dp = (da * dg[rows, col].astype(F32)).astype(BF16)
                    dg[rows, col] = dp
                    dr[rows, :] += dot_nt(dp, wuv[h, :, k * CH : (k + 1) * CH])
                put(ref, 0, dot_nn(hlt[...], dg[:, col]))
                if h is other:
                    begin(c)
            tick()
            begun[c] = 0

    vm = pltpu.VMEM
    ff = 2 * ff_half
    pl.run_scoped(
        feed_forward, vm((full, ff), BF16), vm((full, ff), BF16), vm((full, width), BF16),
        vm((width, full), BF16), vm((2,) + wu.shape, BF16), vm((2,) + wd.shape, BF16),
    )

    def norm_and_out(n1, rs1, ctxv, mav, wov, gov):
        first = load(
            [(n1_i, n1), (rs1_i, rs1), (ma_i, mav), (wo, wov.at[t]), (wo_p, wov.at[other]),
             (ctx_i, ctxv)], 9,
        )
        for cp in first[:3]:
            cp.wait()

        def norm_one_back(b, sums):
            rows = pl.ds(pl.multiple_of(b * 256, 256), 256)
            dh = dr[rows, :]
            n = n1[rows, :]
            g = dh * gain1
            r = (
                g - jnp.mean(g, axis=1, keepdims=True) - n * jnp.mean(g * n, axis=1, keepdims=True)
            ) * rs1[rows, :1]
            dr[rows, :] = r
            g2[rows, :] = (r * (mav[rows, :].astype(F32) * INV_KEEP)).astype(BF16)
            return (
                sums[0] + jnp.sum(dh * n, axis=0, keepdims=True),
                sums[1] + jnp.sum(dh, axis=0, keepdims=True),
            )

        zero = jnp.zeros((1, width), F32)
        gg1, gs1 = lax.fori_loop(0, full // 256, norm_one_back, (zero, zero))
        for i, row in enumerate((gg1, gs1, ng2[0:1, :], ng2[1:2, :])):
            for g in range(groups):
                nsend[i * groups + g : i * groups + g + 1, :] = row[:, g * 128 : (g + 1) * 128]
        nall[me] = nsend[...]
        lax.fori_loop(1, n_dev, lambda k, _: push(k, 0), 0)
        for cp in first[3:]:
            cp.wait()
        lane = lax.broadcasted_iota(jnp.int32, (full, 128), 1)
        seg = (
            (lax.broadcasted_iota(jnp.int32, (128, 128), 0) < 64)
            != (lax.broadcasted_iota(jnp.int32, (128, 128), 1) < 64)
        ).astype(F32).astype(BF16)
        for g in range(groups):
            h, j = g // pairs, g % pairs
            cf = ctxv[g]
            gov[g * 128 : (g + 1) * 128, :] = dot_tn(cf.astype(BF16), g2[...]).astype(BF16)
            dc = dot_nt(g2[...], wov[h, j * 128 : (j + 1) * 128, :]).astype(BF16).astype(F32)
            hi, mid, lo = split_three(dc * cf)
            delta = (
                dot_nn(hi.astype(BF16), seg) + dot_nn(mid.astype(BF16), seg)
                + dot_nn(lo.astype(BF16), seg)
            )
            hi, mid, lo = split_three(delta)
            for a in range(2):
                own = (lane < 64) if a == 0 else (lane >= 64)
                z = 64 if a == 0 else 0
                extra = jnp.where(
                    lane == z, hi,
                    jnp.where(lane == z + 1, mid, jnp.where(lane == z + 2, lo, 0.0)),
                )
                dobv[2 * g + a] = jnp.where(own, dc, extra).astype(BF16)
            if g == pairs - 1:
                tick()
        for j in range(pairs):
            c = 2 * n_cols + j
            for h, ref in ((other, stage.at[c % 3]), (t, mine.at[c])):
                row = pl.ds(pl.multiple_of((h * pairs + j) * 128, 128), 128)
                for g in range(groups):
                    ref[3 * width + g * 128 : 3 * width + (g + 1) * 128, :] = gov[
                        row, g * 128 : (g + 1) * 128
                    ]
        tick()

    def push(k, what):
        lin = lax.rem(me + k, n_dev)
        c = pltpu.make_async_remote_copy(
            src_ref=nsend, dst_ref=nall.at[me], send_sem=nsend_sem.at[k], recv_sem=nrecv_sem.at[me],
            device_id=(lin // 2, lax.rem(lin, 2)), device_id_type=MESH,
        )
        if what == 0:
            c.start()
        else:
            c.wait_send()
        return 0

    def arrive(k, _):
        lin = lax.rem(me + k, n_dev)
        pltpu.make_async_remote_copy(
            src_ref=nsend, dst_ref=nall.at[lin], send_sem=nsend_sem.at[k],
            recv_sem=nrecv_sem.at[lin], device_id=(lin // 2, lax.rem(lin, 2)), device_id_type=MESH,
        ).wait_recv()
        return 0

    pl.run_scoped(
        norm_and_out, vm((full, width), F32), vm((full, 128), F32), vm((groups, full, 128), F32),
        vm((full, width), BF16), vm((2,) + wo.shape, BF16), vm((width, width), BF16),
    )

    def attention(dq3, qbv, qkvv, xv, xt):
        first = load([(qkv_i, qkvv), (qb_i, qbv), (x0_i, xv)], 15)
        length = lens[d]
        lane = lax.broadcasted_iota(jnp.int32, (full, 128), 1)
        bias = jnp.where(
            lax.broadcasted_iota(jnp.int32, (full, 128), 0) < length, 0.0, MASKED_SCORE
        )
        kb = 512
        low_half = lax.broadcasted_iota(jnp.int32, (kb, 128), 1) < 64
        for cp in first:
            cp.wait()
        for g in range(groups):
            cols = slice(g * 128, (g + 1) * 128)
            xt[cols, :] = (xv[:, cols].astype(F32) * INV_KEEP).T.astype(BF16)

        def head_pair(h, j):
            i = h * pairs + j

            def part(c):
                return qkvv[h, :, c * hw + j * 128 : c * hw + (j + 1) * 128]

            k2f = part(1).astype(F32)
            k2t = k2f.T.astype(BF16)
            v2f = part(2).astype(F32)
            dks, dvs, dqs = [], [], []
            for a in range(2):
                own = (lane < 64) if a == 0 else (lane >= 64)
                z = 64 if a == 0 else 0
                minus = jnp.where(jnp.logical_and(lane >= z, lane < z + 3), -1.0, 0.0)
                ka = jnp.where(own, k2f, jnp.where(lane == z + 3, bias, minus)).astype(BF16)
                va = jnp.where(own, v2f, minus).astype(BF16)
                qa = qbv[2 * i + a]
                da = dobv[2 * i + a]
                dk, dv = [], []
                dqt = None
                for b in range(full // kb):
                    rows = slice(b * kb, (b + 1) * kb)
                    p = jnp.exp(dot_nt(ka[rows], qa))
                    ds = (p * dot_nt(va[rows], da)).astype(BF16)
                    dv.append(dot_nn(p.astype(BF16), da))
                    dk.append(dot_nn(ds, qa))
                    term = dot_nn(k2t[a * 64 : (a + 1) * 64, rows], ds)
                    dqt = term if dqt is None else dqt + term
                dks.append(dk)
                dvs.append(dv)
                dqs.append(dqt)
            for b in range(full // kb):
                rows = slice(b * kb, (b + 1) * kb)
                dq3[i, rows, 128:256] = jnp.where(low_half, dks[0][b], dks[1][b]).astype(BF16)
                dq3[i, rows, 256:384] = jnp.where(low_half, dvs[0][b], dvs[1][b]).astype(BF16)
            dq = jnp.concatenate(dqs, axis=0) * HEAD_DIM**-0.5
            dq3[i, :, 0:128] = dq.T.astype(BF16)

        for j in range(pairs):
            c = 2 * n_cols + j
            for h, ref in ((other, stage.at[c % 3]), (t, mine.at[c])):
                head_pair(h, j)
                put(ref, 0, dot_nn(xt[...], dq3[h * pairs + j]))
                if h is other:
                    begin(c)
                tick()
            begun[c] = 0

    def to_input(dq3, wqv, dinv, acc, gtv):
        first = load([(wq_i, wqv), (din_i, dinv)], 18)
        for cp in first:
            cp.wait()

        def d_input(start):
            rows = pl.ds(pl.multiple_of(start, 256), 256)
            total = dr[rows, :]
            for h in range(2):
                lhs = jnp.concatenate(
                    [dq3[h * pairs + j, rows, c * 128 : (c + 1) * 128] for c in range(3) for j in range(pairs)],
                    axis=1,
                )
                total = total + dot_nt(lhs, wqv[h])
            return total

        for s in range(loc // 256):
            gout[s * 256 : (s + 1) * 256, :] = d_input(other * loc + s * 256).astype(BF16)
        send = pltpu.make_async_remote_copy(
            src_ref=gout, dst_ref=gin, send_sem=gt_sem.at[0], recv_sem=gt_sem.at[1],
            device_id=peer, device_id_type=MESH,
        )
        send.start()
        tick()
        for s in range(loc // 256):
            acc[s * 256 : (s + 1) * 256, :] = d_input(t * loc + s * 256)
        tick()
        send.wait()
        for s in range(loc // 256):
            rows = slice(s * 256, (s + 1) * 256)
            gtv[rows, :] = (
                jnp.where(dinv[t, rows, :] != 0, acc[rows, :], 0.0)
                + jnp.where(dinv[other, rows, :] != 0, gin[rows, :].astype(F32), 0.0)
            ) * INV_KEEP
        out = pltpu.make_async_copy(gtv, gt_o, gt_sem.at[2])
        out.start()
        tick()
        lax.fori_loop(1, n_dev, arrive, 0)
        total = nall[0]
        for k in range(1, n_dev):
            total = total + nall[k]
        ng_o[...] = total
        tick()
        while any(a <= 2 * bits for a in begun.values()):
            tick()
        out.wait()

    def projections(dq3):
        pl.run_scoped(
            functools.partial(attention, dq3), vm((2 * groups, full, 128), BF16),
            vm(qkv_i.shape, BF16), vm((full, width), BF16), vm((width, full), BF16),
        )
        pl.run_scoped(
            functools.partial(to_input, dq3), vm(wq_i.shape, BF16), vm(din_i.shape, jnp.int32),
            vm((loc, width), F32), vm((loc, width), F32),
        )

    pl.run_scoped(projections, vm((groups, full, 384), BF16))
    for c in range(n_chunks):
        for cp in out_copies(c):
            cp.wait()
    lax.fori_loop(1, n_dev, lambda k, _: push(k, 1), 0)


def back(
    lengths, vecs, ng2, g2, dr2, act, dg, hl, n1, rs1, ctx, ma, wo, wo_p, wu, wu_p, wd, wd_p, qb,
    qkv, x0, wq, d_in, n_dp,
):
    full, width = x0.shape
    loc = full // 2
    groups = width // 128
    bits = n_dp.bit_length() - 1
    n_dev = 2 * n_dp
    n_chunks = 2 * (wu.shape[1] // CH) + groups // 2
    rows_c = CH * width // 128
    sds = jax.ShapeDtypeStruct
    anyspec = pl.BlockSpec(memory_space=pl.ANY)
    vspec = pl.BlockSpec(memory_space=pltpu.VMEM)
    vm = pltpu.VMEM
    dma = pltpu.SemaphoreType.DMA
    return pl.pallas_call(
        back_kernel,
        out_shape=[
            sds(wq.shape[1:], BF16), sds(wo.shape, BF16), sds(wu.shape, BF16), sds(wd.shape, BF16),
            sds((loc, width), F32), sds((4 * groups, 128), F32),
        ],
        in_specs=[pl.BlockSpec(memory_space=pltpu.SMEM), vspec, vspec] + [anyspec] * 20,
        out_specs=[anyspec] * 5 + [vspec],
        scratch_shapes=[
            vm((n_chunks, rows_c, 128), BF16), vm((n_chunks, rows_c, 128), BF16),
            vm((n_chunks, rows_c, 128), BF16), vm((3, rows_c, 128), BF16),
            vm((full, width), BF16), vm((full, width), F32), vm(qb.shape, BF16),
            vm((loc, width), BF16), vm((loc, width), BF16),
            vm((4 * groups, 128), F32), vm((n_dev, 4 * groups, 128), F32),
            dma((20,)), dma((n_chunks,)), dma((n_chunks,)), dma((n_chunks, 2 * bits)),
            dma((n_chunks, 2 * bits)), dma((n_chunks, 9)), dma((n_dev,)), dma((n_dev,)), dma((3,)),
        ],
        compiler_params=pltpu.CompilerParams(
            collective_id=2, has_side_effects=True, vmem_limit_bytes=VMEM_LIMIT
        ),
        name="back",
    )(
        lengths, vecs, ng2, g2, dr2, act, dg, hl, n1, rs1, ctx, ma, wo, wo_p, wu, wu_p, wd, wd_p,
        qb, qkv, x0, wq, d_in,
    )


def per_device(
    tokens, lengths, drop_in, drop_attn, drop_ffn, qkv_weight, out_weight, up_weight, down_weight,
    gain_first, shift_first, gain_second, shift_second, cotangent,
):
    n_dp = lax.axis_size("dp")
    width = tokens.shape[2]
    wq = qkv_weight.reshape(width, -1)
    x0, ma, mf, cot_p, wqf, wo_p, wu_p, wd_p, qkv, qb, ctx = front(
        lengths, tokens[0], drop_in[0], drop_attn[0], drop_ffn[0], cotangent[0],
        wq, out_weight, up_weight, down_weight,
    )
    lens_b = jnp.broadcast_to(lengths.astype(F32)[:, None], (n_dp, 128))
    vecs = jnp.stack([gain_first, shift_first, gain_second, shift_second] * 2)
    lay, stats, act, dg, hl, n1, rs1, g2, dr2, ng2 = middle(
        lengths, lens_b, vecs, ctx, x0, ma, mf, cotangent[0], cot_p, out_weight, wo_p,
        up_weight, wu_p, down_weight, wd_p, n_dp,
    )
    gq, go, gu, gd, gt, norms = back(
        lengths, vecs, ng2, g2, dr2, act, dg, hl, n1, rs1, ctx, ma, out_weight, wo_p,
        up_weight, wu_p, down_weight, wd_p, qb, qkv, x0, wqf, drop_in[0], n_dp,
    )
    norms = norms.reshape(4, width)
    return (
        lay[None], gt[None], gq.reshape(qkv_weight.shape).astype(F32), go.astype(F32),
        gu.astype(F32), gd.astype(F32),
        norms[0], norms[1], norms[2], norms[3],
        stats[0, 0], stats[1, 0], stats[2, 0],
    )


def solution(mesh):
    act = P("dp", None, "tensor", None)
    in_specs = (
        P("dp", "tensor", None), P(), act, act, act,
        P(None, None, "tensor"), P("tensor", None), P(None, "tensor"), P("tensor", None),
        P(), P(), P(), P(), act,
    )
    out_specs = (
        act, P("dp", "tensor", None),
        P(None, None, "tensor"), P("tensor", None), P(None, "tensor"), P("tensor", None),
        P(), P(), P(), P(), P(), P(), P(),
    )
    return jax.shard_map(
        per_device, mesh=mesh, in_specs=in_specs, out_specs=out_specs, check_vma=False
    )
```

time: 708 us -> 317 us (0.45)
  waiting for transfers between devices: 242 us -> 0 us
  Pallas kernels: 371 us -> 280 us
  blocking collectives: 42.9 us -> 0 us
  between operations: 14.3 us -> 1.13 us
    pallas_call x1, Pallas kernels: 243 us -> 34.5 us  [front(): pl.pallas_call(front_kernel, out_shape=outs, in_specs=[pl.BlockSpec(memor...]
    psum x1 -> x0, waiting for transfers between devices: 192 us -> none  [per_device(): summed.append(lax.psum(g, 'dp').astype(F32))]
    pallas_call x1, Pallas kernels: 48.9 us -> 200 us  [back(): pl.pallas_call(back_kernel, out_shape=[sds(wq.shape[1:], BF16), sds(wo.sh...]
    reduce_scatter x4 -> x0, waiting for transfers between devices: 48.1 us -> none  [per_device(): g = lax.psum_scatter(g, 'tensor', scatter_dimension=0, tiled=False)]
    psum x1 -> x0, blocking collectives: 42.9 us -> none  [per_device(): norms = lax.psum(ng, ('dp', 'tensor'))]
    pallas_call x1, Pallas kernels: 79.1 us -> 45.6 us  [middle(): pl.pallas_call(middle_kernel, out_shape=outs, in_specs=[pl.BlockSpec(memo...]
  transfers between devices with their start and end apart: 5 -> 0, of which waited for: 5 -> 0; matrix products, arithmetic and copies ran while one was open for 1% -> 0% of each run, Pallas kernels for 0% -> 0%
where the time goes in v2:
time: 317 us; the launch traced here: 311 us
  Pallas kernels  280 us (88%)
  local copies, waits for them, and re-layouts  20.3 us (6%)
  other arithmetic  10 us (3%)
    pallas_call x1, Pallas kernels, back(): pl.pallas_call(back_kernel, out_shape=[sds(wq.shape[1:], BF16), sds(wo.sh...  200 us
    pallas_call x1, Pallas kernels, middle(): pl.pallas_call(middle_kernel, out_shape=outs, in_specs=[pl.BlockSpec(memo...  45.6 us
    pallas_call x1, Pallas kernels, front(): pl.pallas_call(front_kernel, out_shape=outs, in_specs=[pl.BlockSpec(memor...  34.5 us
    unnamed x10, local copies, waits for them, and re-layouts  8.69 us

profile of v2, /device:TPU:0, one launch (start us, length us, event | category | flops | bytes accessed | tf_op | source)
XLA Modules:
  0.0 311.1 jit_solution(17354798429465348828)
XLA Ops:
  0.6 0.7 convert_element_type.18
  1.3 0.7 stack.19
  2.0 0.7 stack.20
  2.7 0.7 stack.21
  3.4 0.7 stack.22
  4.1 0.7 broadcast_in_dim.12.lens_b
  4.7 0.6 stack.23.vecs
  5.4 2.6 copy.29
  8.0 2.2 copy.30.wq
  10.2 34.5 %front.1 = (bf16[1024,768]{1,0:T(8,128)(2,1)}, bf16[1024,768]{1,0:T(8,128)(2,1)}, bf16[1024,768]{1,0:T(8,128)(2,1)}, bf16[512,768]{1,0:T(8,128)(2,1)}, bf16[2,76...) custom-call(s32[16]{0:T(128)} %lens.5, ...), custom_call_target="tpu_custom_call" | custom-call | tf_op jit(solution)/shard_map/front/pallas_call | solution.py:246
  44.7 45.6 %middle.1 = (bf16[2,512,768]{2,1,0:T(8,128)(2,1)}, f32[8,128]{1,0:T(8,128)}, bf16[1024,3072]{1,0:T(8,128)(2,1)}, bf16[1024,3072]{1,0:T(8,128)(2,1)}, bf16[1024,7...) custom-call(s32[16]{0:T(128)} %lens.5, ...), custom_call_target="tpu_custom_call" | custom-call | tf_op jit(solution)/shard_map/middle/pallas_call | solution.py:520
  90.3 199.6 %back.1 = (bf16[768,1152]{1,0:T(8,128)(2,1)}, bf16[384,768]{1,0:T(8,128)(2,1)}, bf16[768,1536]{1,0:T(8,128)(2,1)}, bf16[1536,768]{1,0:T(8,128)(2,1)}, f32[512,768]{1,0:T(8,128)}, /*index=5*/f32[24,128]{1,0:T(8,128)}) custom-call(s32[16]{0:T(128)} %lens.5, f32[8,768]{1,0:T(8,128)} %stack.23.vecs, f32[8,768]{1,0:T(8,128)} %get-tuple-element.49.ng2, ...), custom_call_target="tpu_custom_call" | custom-call | tf_op jit(solution)/shard_map/back/pallas_call | solution.py:994
  290.0 1.3 fusion
  291.3 1.4 slice_bitcast_fusion
  292.6 2.2 convert_element_type.21
  294.8 2.6 copy.31
  297.4 2.9 copy.32
  300.4 4.6 %convert_element_type.22 = f32[768,1536]{1,0:T(8,128)} convert(bf16[768,1536]{1,0:T(8,128)(2,1)} %get-tuple-element.63) | non-fusion elementwise | flops 1179648 | bytes 7077888 | tf_op jit(solution)/shard_map/convert_element_type | solution.py:1045
  305.0 0.0 copy-done
  305.0 2.5 convert_element_type.23
  307.6 0.0 copy-done.1
  307.6 1.1 copy.35
  308.7 0.8 copy-done.2
  309.6 1.1 copy.36
  (3 shorter events, 0.0 us)
Async XLA Ops:
  300.4 4.7 %copy-start = (bf16[1536,768]{1,0:T(8,128)(2,1)S(1)}, bf16[1536,768]{1,0:T(8,128)(2,1)}, u32[]{:S(2)}) copy-start(bf16[1536,768]{1,0:T(8,128)(2,1)} %get-tuple-element.64) | copy-start | bytes 7077892
  305.0 2.5 copy-start.1
  307.6 2.0 copy-start.2
